TPU v7x, 256 devices: a whole 4x4x8 slice. The times are simulated.
256 devices in a mesh: blk: 32 (over x, z), grp: 8 (over y, core).
Axes of the slice: x: 4, y: 4, z: 8, core: 2. Of those that a mesh axis runs over, the one named last changes fastest.
Arguments:
- features: bfloat16 [8, 8192, 256], P('grp', 'blk'), may hold values from -6 to 6
- weight: bfloat16 [256, 256], replicated, may hold values from -0.375 to 0.375
- cotangent: bfloat16 [8, 8192, 256], P('grp', 'blk'), may hold values from -6 to 6
- dense_tiles: bfloat16 [8, 32, 64, 128, 128], P('grp', 'blk'), as said below
- dense_cols: int32 [8, 32, 64], P('grp', 'blk'), may hold values from 0 to 1, as said below
- sparse_tiles: bfloat16 [8, 32, 32, 128, 128], P('grp', 'blk'), may hold values from -0.09375 to 0.09375
- sparse_rows: int32 [8, 32, 32], P('grp', 'blk'), may hold values from 0 to 1
- sparse_cols: int32 [8, 32, 32], P('grp', 'blk'), may hold values from 0 to 7
- send_rows: int32 [8, 32, 8, 128], P('grp', 'blk'), may hold values from 0 to 255
- send_counts: int32 [8, 32, 8], P('grp', 'blk'), may hold values from 16 to 128, as said below
Outputs:
- hidden: bfloat16 [8, 8192, 256], P('grp', 'blk')
- grad_features: bfloat16 [8, 8192, 256], P('grp', 'blk')
- grad_weight: float32 [256, 256], replicated
Inputs may be any that keep to these rules, and one draw needn't show every extreme that they name: Tile t of device (g, b) has row tile t % 2 and source block t // 2; for one device and one source block the 2 tiles name distinct column tiles, and the adjacency given by dense_tiles and dense_cols inside each group is symmetric. `dense_tiles`: together with dense_cols the tiles give a symmetric adjacency inside each group. `send_counts`: entry [s, b, g] counts the rows that device (s, b) sends to device (g, b); for every block index some receiver gets 128 rows from every sender.
All inputs are finite; a program needn't handle non-finite values.
Results may differ from a plain program's by a relative error of at most 0.0065.
Values may be sent and summed in bfloat16 or wider, within the bound.
No kernel may reach another device: no remote copies, remote signals or barrier semaphores. Data moves between devices by JAX's collectives and lax.ppermute only.
A program may use at most 64 MiB of HBM per device.

v0:
```python
import jax
import jax.numpy as jnp
from jax import lax
from jax.sharding import PartitionSpec as P


def body(
    features,
    weight,
    cotangent,
    dense_tiles,
    dense_cols,
    sparse_tiles,
    sparse_rows,
    sparse_cols,
    send_rows,
    send_counts,
):
    row_count = features.shape[1]
    hidden_width = weight.shape[1]
    tile_values = dense_tiles[0, 0]
    tile_cols = dense_cols[0, 0]
    tile_size = tile_values.shape[-1]
    row_tiles = row_count // tile_size
    projected = jnp.dot(features[0], weight, preferred_element_type=jnp.float32).astype(
        jnp.bfloat16
    )
    send_list = send_rows[0, 0]
    send_count = send_counts[0, 0]
    capacity = send_list.shape[1]
    in_use = jnp.arange(capacity)[None, :] < send_count[:, None]
    outgoing = jnp.where(in_use[:, :, None], projected[send_list], jnp.zeros((), jnp.bfloat16))
    received = lax.all_to_all(outgoing, "grp", split_axis=0, concat_axis=0, tiled=True)
    shards = lax.all_gather(projected, "blk", axis=0, tiled=True)
    block_count = shards.shape[0] // row_count
    chosen = tile_values
    chosen_cols = tile_cols
    positions = jnp.arange(block_count * row_tiles) // row_tiles * row_tiles + chosen_cols
    source = shards.reshape(block_count * row_tiles, tile_size, hidden_width)[positions]
    dense_part = jnp.einsum(
        "crij,crjh->rih",
        chosen.reshape(block_count, row_tiles, tile_size, tile_size),
        source.reshape(block_count, row_tiles, tile_size, hidden_width),
        preferred_element_type=jnp.float32,
    )
    sparse_vals = sparse_tiles[0, 0]
    row_slot = sparse_rows[0, 0]
    col_block = sparse_cols[0, 0]
    recv_count = received.shape[0]
    products = jnp.einsum(
        "uij,ujh->uih", sparse_vals, received[col_block], preferred_element_type=jnp.float32
    )
    row_pick = (row_slot[:, None] == jnp.arange(row_tiles)[None, :]).astype(jnp.float32)
    sparse_part = jnp.einsum("ur,uih->rih", row_pick, products, precision=lax.Precision.HIGHEST)
    pre_act = (dense_part + sparse_part).reshape(row_count, hidden_width)
    sigmoid_pre = jax.nn.sigmoid(pre_act)
    hidden = (pre_act * sigmoid_pre).astype(jnp.bfloat16)
    grad_pre = (
        cotangent[0].astype(jnp.float32) * sigmoid_pre * (1.0 + pre_act * (1.0 - sigmoid_pre))
    ).astype(jnp.bfloat16)
    grad_tiles = grad_pre.reshape(row_tiles, tile_size, hidden_width)
    block_count = row_count * lax.axis_size("blk") // row_count
    chosen = tile_values
    chosen_cols = tile_cols
    chosen = chosen.reshape(block_count, row_tiles, tile_size, tile_size)
    chosen_cols = chosen_cols.reshape(block_count, row_tiles)
    moved = jnp.einsum("crij,rih->crjh", chosen, grad_tiles, preferred_element_type=jnp.float32)
    pieces = [
        jnp.sum(jnp.where((chosen_cols == target)[:, :, None, None], moved, 0.0), axis=1)
        for target in range(row_tiles)
    ]
    dense_back = lax.psum_scatter(
        jnp.stack(pieces, axis=1).reshape(row_count * lax.axis_size("blk"), hidden_width),
        "blk",
        scatter_dimension=0,
        tiled=True,
    )
    tile_grads = jnp.einsum(
        "uij,uih->ujh", sparse_vals, grad_tiles[row_slot], preferred_element_type=jnp.float32
    )
    block_pick = (col_block[:, None] == jnp.arange(recv_count)[None, :]).astype(jnp.float32)
    slot_grad = jnp.einsum("uq,ujh->qjh", block_pick, tile_grads, precision=lax.Precision.HIGHEST)
    returned = lax.all_to_all(slot_grad, "grp", split_axis=0, concat_axis=0, tiled=True)
    returned = jnp.where(in_use[:, :, None], returned, 0.0)
    sparse_back = (
        jnp.zeros((row_count, hidden_width), jnp.float32)
        .at[send_list.reshape(-1)]
        .add(returned.reshape(-1, hidden_width))
    )
    agg_grad = (dense_back + sparse_back).astype(jnp.bfloat16)
    grad_features = jnp.einsum(
        "rh,fh->rf", agg_grad, weight, preferred_element_type=jnp.float32
    ).astype(jnp.bfloat16)
    partial_weight = jnp.einsum(
        "rf,rh->fh", features[0], agg_grad, preferred_element_type=jnp.float32
    )
    vertex_total = row_count * lax.axis_size("blk") * lax.axis_size("grp")
    grad_weight = lax.psum(partial_weight, ("blk", "grp")) * float(vertex_total) ** (-0.5)
    return (hidden[None], grad_features[None], grad_weight)


def solution(mesh):
    placed = (
        P("grp", "blk", None),
        P(),
        P("grp", "blk", None),
        P("grp", "blk", None, None, None),
        P("grp", "blk", None),
        P("grp", "blk", None, None, None),
        P("grp", "blk", None),
        P("grp", "blk", None),
        P("grp", "blk", None, None),
        P("grp", "blk", None),
    )
    return jax.shard_map(
        body,
        mesh=mesh,
        in_specs=placed,
        out_specs=(P("grp", "blk", None), P("grp", "blk", None), P()),
        check_vma=False,
    )
```

profile of v0, /device:TPU:1, one launch (start us, length us, event | category | flops | bytes accessed | tf_op | source)
XLA Modules:
  0.0 612.8 jit_solution(7899231333244268528)
XLA Ops:
  7.3 1.9 convolution_convert_fusion.1
  9.9 4.4 gather_fusion.1
  15.4 6.6 %all-to-all-start = ((bf16[8,128,256]{2,1,0:T(8,128)(2,1)}), bf16[8,128,256]{2,1,0:T(8,128)(2,1)S(1)}, u32[]{:S(2)}, u32[]{:S(2)}) async-start(bf16[8,128,256]{2,1,0:T(8,128)(2,1)} %broadcast_select_fusion.1), calls=%async_computation | async-start | bytes 1048576 | tf_op jit(solution)/shard_map/all_to_all | solution.py:33
  22.6 9.0 %all-to-all-done = bf16[8,128,256]{2,1,0:T(8,128)(2,1)S(1)} async-done(((bf16[8,128,256]{2,1,0:T(8,128)(2,1)}), bf16[8,128,256]{2,1,0:T(8,128)(2,1)S(1)}, u32[]{:S(2)}, u32[]{:S(2)}) %all-to-all-start) | async-done | bytes 524320 | tf_op jit(solution)/shard_map/all_to_all | solution.py:33
  31.6 2.0 gather_fusion.2
  33.6 4.6 convolution_bitcast_fusion.1
  38.2 5.5 copy.32
  43.7 3.6 fusion.25
  47.3 46.9 %all-gather.2.cloned.1.call-done = bf16[8192,256]{1,0:T(8,128)(2,1)} async-done(((bf16[256,256]{1,0:T(8,128)(2,1)}), bf16[8192,256]{1,0:T(8,128)(2,1)}) %all-gather.2.cloned.1.call-update) | async-done | bytes 4194320 | tf_op jit(solution)/shard_map/all_gather | solution.py:34
  94.1 5.0 gather_fusion
  99.1 3.0 fusion.9
  102.1 3.4 fusion
  105.5 3.8 pad_maximum_fusion
  109.3 9.0 %copy.38 = f32[32,2,128,256]{3,2,1,0:T(8,128)} copy(f32[32,2,128,256]{2,3,0,1:T(8,128)} %pad_maximum_fusion) | data formatting | bytes 16777216 | tf_op jit(solution)/shard_map/stack | solution.py:73
  118.3 2.0 gather_fusion.3
  120.3 4.3 convolution_bitcast_fusion
  124.6 5.5 copy.40
  130.1 3.7 fusion.22
  135.1 7.6 %all-to-all-start.1 = ((f32[8,128,256]{2,1,0:T(8,128)}), f32[8,128,256]{2,1,0:T(8,128)}, u32[]{:S(2)}, u32[]{:S(2)}) async-start(f32[8,128,256]{2,1,0:T(8,128)} %copy.41), calls=%async_computation.2 | async-start | bytes 2097152 | tf_op jit(solution)/shard_map/all_to_all | solution.py:83
  142.7 15.2 %all-to-all-done.1 = f32[8,128,256]{2,1,0:T(8,128)} async-done(((f32[8,128,256]{2,1,0:T(8,128)}), f32[8,128,256]{2,1,0:T(8,128)}, u32[]{:S(2)}, u32[]{:S(2)}) %all-to-all-start.1) | async-done | bytes 1048608 | tf_op jit(solution)/shard_map/all_to_all | solution.py:83
  159.3 184.2 %reduce-scatter.2.cloned.1.call-done = f32[256,256]{1,0:T(8,128)} async-done(((f32[8192,256]{1,0:T(8,128)}), f32[256,256]{1,0:T(8,128)}) %reduce-scatter.2.cloned.1.call-update) | async-done | bytes 262160 | tf_op jit(solution)/shard_map/reduce_scatter | solution.py:72
  343.5 7.7 %scatter_fusion = f32[256,256]{1,0:T(8,128)} fusion(f32[256,256]{1,0:T(8,128)} %reduce-scatter.2.cloned.1.call-done, s32[1024]{0:T(1024)S(1)} %bitcast.110, f32[1024,256]{1,0:T(8,128)S(1)} %bitcast.103), kind=kCustom, calls=%fused_computation.4 | custom fusion | flops 262144 | bytes 3149824 | tf_op jit(solution)/shard_map/scatter-add | solution.py:88
  351.2 1.9 convolution_bitcast_fusion.3
  355.7 248.8 %all-reduce.2.cloned.1.call-done = f32[256,256]{0,1:T(8,128)} async-done(((f32[256,256]{0,1:T(8,128)}), f32[256,256]{0,1:T(8,128)}) %all-reduce.2.cloned.1.call-update) | async-done | bytes 262160 | tf_op jit(solution)/shard_map/psum | solution.py:98
  (45 shorter events, 9.5 us)
Async XLA Ops:
  7.2 92.0 %copy-start = (bf16[1,1,64,128,128]{4,3,2,1,0:T(8,128)(2,1)S(1)}, bf16[1,1,64,128,128]{4,3,2,1,0:T(8,128)(2,1)}, u32[]{:S(2)}) copy-start(bf16[1,1,64,128,128]{4,3,2,1,0:T(8,128)(2,1)} %param.13) | copy-start | bytes 6291460
  7.2 7.1 %copy-start.7 = (s32[1,1,8]{2,1,0:T(1,128)S(1)}, s32[1,1,8]{2,1,0:T(1,128)}, u32[]{:S(2)}) copy-start(s32[1,1,8]{2,1,0:T(1,128)} %param.19) | copy-start | bytes 100
  7.2 14.9 %copy-start.6 = (s32[1,1,32]{2,1,0:T(1,128)S(1)}, s32[1,1,32]{2,1,0:T(1,128)}, u32[]{:S(2)}) copy-start(s32[1,1,32]{2,1,0:T(1,128)} %param.17) | copy-start | bytes 388
  7.2 14.9 %copy-start.8 = (s32[1,1,64]{2,1,0:T(1,128)S(1)}, s32[1,1,64]{2,1,0:T(1,128)}, u32[]{:S(2)}) copy-start(s32[1,1,64]{2,1,0:T(1,128)} %param.14) | copy-start | bytes 772
  7.2 86.9 %all-gather.2.cloned.1.call-start = ((), (), s32[]{:S(2)}) async-start(), calls=%async_computation.3 | async-start | bytes 4325376 | tf_op jit(solution)/shard_map/all_gather | solution.py:34
  15.4 16.1 %all-to-all-start = ((bf16[8,128,256]{2,1,0:T(8,128)(2,1)}), bf16[8,128,256]{2,1,0:T(8,128)(2,1)S(1)}, u32[]{:S(2)}, u32[]{:S(2)}) async-start(bf16[8,128,256]{2,1,0:T(8,128)(2,1)} %broadcast_select_fusion.1), calls=%async_computation | async-start | bytes 1048576 | tf_op jit(solution)/shard_map/all_to_all | solution.py:33
  22.1 321.4 %reduce-scatter.2.cloned.1.call-start = ((), (), s32[]{:S(2)}) async-start(), calls=%async_computation.4 | async-start | bytes 8650752 | tf_op jit(solution)/shard_map/reduce_scatter | solution.py:72
  38.2 5.5 copy-start.5
  94.1 5.0 copy-start.3
  118.3 2.1 copy-start.1
  130.1 12.6 %copy-start.4 = (s32[1,1,8,128]{3,2,1,0:T(8,128)S(1)}, s32[1,1,8,128]{3,2,1,0:T(8,128)}, u32[]{:S(2)}) copy-start(s32[1,1,8,128]{3,2,1,0:T(8,128)} %param.18) | copy-start | bytes 12292
  135.1 22.8 %all-to-all-start.1 = ((f32[8,128,256]{2,1,0:T(8,128)}), f32[8,128,256]{2,1,0:T(8,128)}, u32[]{:S(2)}, u32[]{:S(2)}) async-start(f32[8,128,256]{2,1,0:T(8,128)} %copy.41), calls=%async_computation.2 | async-start | bytes 2097152 | tf_op jit(solution)/shard_map/all_to_all | solution.py:83
  142.6 461.9 %all-reduce.2.cloned.1.call-start = ((), (), s32[]{:S(2)}) async-start(), calls=%async_computation.5 | async-start | bytes 524288 | tf_op jit(solution)/shard_map/psum | solution.py:98
  343.5 7.7 %copy-start.2 = (bf16[1,256,256]{2,1,0:T(8,128)(2,1)S(1)}, bf16[1,256,256]{2,1,0:T(8,128)(2,1)}, u32[]{:S(2)}) copy-start(bf16[1,256,256]{2,1,0:T(8,128)(2,1)} %param.10) | copy-start | bytes 393220
Sparse Core Ops, SparseCore 0:
  11.2 82.8 all-gather.1
  118.4 225.0 reduce-scatter.1
  353.2 251.2 all-reduce.1
where the time goes:
time: 614 us; the launch traced here: 613 us
  waiting for transfers between devices  504 us (82%)
  local copies, waits for them, and re-layouts  36 us (6%)
  matrix products  28.2 us (5%)
  other arithmetic  16.4 us (3%)
  starting transfers between devices  14.2 us (2%)
  between operations  13.9 us (2%)
    psum x1, waiting for transfers between devices, body(): lax.psum(partial_weight, ('blk', 'grp')) * float(vertex_total) ** (-0.5)  249 us
    reduce_scatter x1, waiting for transfers between devices, body(): lax.psum_scatter(jnp.stack(pieces, axis=1).reshape(row_count * lax.axis_s...  184 us
    all_gather x1, waiting for transfers between devices, body(): shards = lax.all_gather(projected, 'blk', axis=0, tiled=True)  46.9 us
    all_to_all x1, waiting for transfers between devices, body(): lax.all_to_all(slot_grad, 'grp', split_axis=0, concat_axis=0, tiled=True)  15.2 us
  transfers between devices with their start and end apart: 5, of which 5 were waited for; matrix products, arithmetic and copies ran while one was open for 7% of the time, Pallas kernels for 0%

commit v1 on v0

v1 whole, which is shorter than its diff:
```python
import functools

import jax
import jax.numpy as jnp
from jax import lax
from jax.experimental import pallas as pl
from jax.experimental.pallas import tpu as pltpu
from jax.sharding import PartitionSpec as P

NX, NZ = 4, 8
TILE = 128
BF = jnp.bfloat16
F32 = jnp.float32
VMEM_LIMIT = 40 * 1024 * 1024


def swap_z(kind):
    def partner(z):
        if kind == 0:
            return z ^ 1
        return (z - 1) % NZ if z % 2 == 0 else (z + 1) % NZ

    return [(x * NZ + z, x * NZ + partner(z)) for x in range(NX) for z in range(NZ)]


def swap_x(kind):
    def partner(x):
        if kind == 0:
            return x ^ 1
        return (x - 1) % NX if x % 2 == 0 else (x + 1) % NX

    return [(x * NZ + z, partner(x) * NZ + z) for x in range(NX) for z in range(NZ)]


def go_z(v, kind):
    return lax.ppermute(v, "blk", swap_z(kind))


def go_x(v, kind):
    return lax.ppermute(v, "blk", swap_x(kind))


def ring_z(v):
    out = [v]
    up, down = go_z(v, 0), go_z(v, 1)
    out += [up, down]
    for _ in range(2):
        up, down = go_z(down, 0), go_z(up, 1)
        out += [up, down]
    h = v.shape[0] // 2
    last = jnp.concatenate([go_z(down[:h], 0), go_z(up[h:], 1)])
    return out + [last]


def ring_x(v):
    up, down = go_x(v, 0), go_x(v, 1)
    h = v.shape[0] // 2
    return [v, up, down, go_x(down[:h], 0), go_x(up[h:], 1)]


def gather(v):
    first = ring_z(jnp.concatenate(ring_x(v[:TILE])))
    second = ring_x(jnp.concatenate(ring_z(v[TILE:])))
    return first + second


def dot(a, b, ca=1, cb=0):
    return lax.dot_general(a, b, (((ca,), (cb,)), ((), ())), preferred_element_type=F32)


def select_kernel(count_ref, rows_ref, x_ref, sel_ref, out_ref):
    lane = lax.broadcasted_iota(jnp.int32, (1, TILE), 1)
    row = lax.broadcasted_iota(jnp.int32, (2 * TILE, TILE), 0)
    for s in range(rows_ref.shape[0]):
        listed = jnp.where(lane < count_ref[s], rows_ref[s : s + 1, :], -1)
        sel = jnp.where(row == listed, 1.0, 0.0).astype(BF)
        sel_ref[:, s * TILE : (s + 1) * TILE] = sel
        out_ref[s] = dot(sel, x_ref[...], 0, 0).astype(BF)


def dense_kernel(place_ref, cols_ref, tiles_ref, out_ref):
    x, z = place_ref[0], place_ref[1]
    sx, sz = 1 - 2 * (x % 2), 1 - 2 * (z % 2)
    zero = jnp.zeros((TILE, TILE), BF)
    zs = [lax.rem(z + NZ + k * sz, NZ) for k in (0, 1, -1, 2, -2, 3, -3, 4)]
    xs = [lax.rem(x + NX + k * sx, NX) for k in (0, 1, -1, 2)]
    slots = [(xv, zv, 0) for zv in zs for xv in xs] + [(xv, zv, 1) for xv in xs for zv in zs]
    for i, (xv, zv, half) in enumerate(slots):
        block = xv * NZ + zv
        r = jnp.where(cols_ref[2 * block] == half, 0, 1)
        tile = tiles_ref[2 * block + r]
        cols = slice(i * TILE, (i + 1) * TILE)
        out_ref[:TILE, cols] = jnp.where(r == 0, tile, zero)
        out_ref[TILE:, cols] = jnp.where(r == 1, tile, zero)


def sparse_kernel(rows_ref, cols_ref, tiles_ref, out_ref, total):
    total[...] = jnp.zeros_like(total)
    for u in range(tiles_ref.shape[0]):
        at = rows_ref[u] * 8 + cols_ref[u]
        total[at] += tiles_ref[u].astype(F32)
    for r in range(2):
        for q in range(8):
            value = total[r * 8 + q]
            high = value.astype(BF)
            low = (value - high.astype(F32)).astype(BF)
            rows = slice(r * TILE, (r + 1) * TILE)
            out_ref[rows, q * TILE : (q + 1) * TILE] = high
            out_ref[rows, (8 + q) * TILE : (9 + q) * TILE] = low


def split(v):
    high = v.astype(BF)
    return high, (v - high.astype(F32)).astype(BF)


def dense_product(a_ref, pieces):
    total, at = None, 0
    for p in pieces:
        n = p.shape[0]
        term = dot(a_ref[:, at : at + n], p[...])
        total = term if total is None else total + term
        at += n
    return total


def forward_kernel(n, *refs):
    a_ref, s_ref, rec_ref, w_ref, cot_ref = refs[:5]
    pieces = refs[5 : 5 + n]
    hidden_ref, grad_ref, slot_ref, pw_ref = refs[5 + n :]
    half = s_ref.shape[1] // 2
    agg = dense_product(a_ref, pieces)
    agg += dot(s_ref[:, :half], rec_ref[...]) + dot(s_ref[:, half:], rec_ref[...])
    high, low = split(agg)
    pre = dot(high, w_ref[...]) + dot(low, w_ref[...])
    sig = jax.nn.sigmoid(pre)
    hidden_ref[...] = (pre * sig).astype(BF)
    grad = (cot_ref[...].astype(F32) * sig * (1.0 + pre * (1.0 - sig))).astype(BF)
    grad_ref[...] = grad
    slot_ref[...] = (dot(s_ref[:, :half], grad, 0, 0) + dot(s_ref[:, half:], grad, 0, 0)).astype(BF)
    pw_ref[...] = dot(high, grad, 0, 0) + dot(low, grad, 0, 0)


def backward_kernel(n, *refs):
    a_ref, sel_ref, ret_ref, w_ref = refs[:4]
    pieces = refs[4 : 4 + n]
    (out_ref,) = refs[4 + n :]
    agg = dense_product(a_ref, pieces) + dot(sel_ref[...], ret_ref[...])
    out_ref[...] = dot(agg.astype(BF), w_ref[...], 1, 1).astype(BF)


SMEM = pl.BlockSpec(memory_space=pltpu.SMEM)
VMEM = pl.BlockSpec(memory_space=pltpu.VMEM)


def call(kernel, ins, outs, scalars=0, scratch=(), name=None, flops=0):
    many = isinstance(outs, list)
    moved = sum(v.size * v.dtype.itemsize for v in list(ins) + (outs if many else [outs]))
    return pl.pallas_call(
        kernel,
        out_shape=outs,
        in_specs=[SMEM] * scalars + [VMEM] * (len(ins) - scalars),
        out_specs=[VMEM] * len(outs) if many else VMEM,
        scratch_shapes=list(scratch),
        compiler_params=pltpu.CompilerParams(vmem_limit_bytes=VMEM_LIMIT),
        cost_estimate=pl.CostEstimate(flops=flops, bytes_accessed=moved, transcendentals=0),
        name=name,
    )(*ins)


def body(
    features,
    weight,
    cotangent,
    dense_tiles,
    dense_cols,
    sparse_tiles,
    sparse_rows,
    sparse_cols,
    send_rows,
    send_counts,
):
    shape = jax.ShapeDtypeStruct
    own = features[0]
    blk = lax.axis_index("blk")
    place = jnp.stack([blk // NZ, blk % NZ]).astype(jnp.int32)
    sel, outgoing = call(
        select_kernel,
        [send_counts[0, 0], send_rows[0, 0], own],
        [shape((256, 1024), BF), shape((8, TILE, 256), BF)],
        scalars=1,
        name="select",
        flops=2 * 1024 * 256 * 256,
    )
    received = lax.all_to_all(outgoing, "grp", 0, 0, tiled=True).reshape(1024, 256)
    pieces = gather(own)
    dense = call(
        dense_kernel,
        [place, dense_cols[0, 0], dense_tiles[0, 0]],
        shape((256, 64 * TILE), BF),
        scalars=2,
        name="dense",
    )
    sparse = call(
        sparse_kernel,
        [sparse_rows[0, 0], sparse_cols[0, 0], sparse_tiles[0, 0]],
        shape((256, 2048), BF),
        scalars=2,
        scratch=[pltpu.VMEM((16, TILE, TILE), F32)],
        name="sparse",
    )
    hidden, grad, slots, partial = call(
        functools.partial(forward_kernel, len(pieces)),
        [dense, sparse, received, weight, cotangent[0]] + pieces,
        [shape((256, 256), BF), shape((256, 256), BF), shape((1024, 256), BF), shape((256, 256), F32)],
        name="forward",
        flops=2 * 256 * 8192 * 256,
    )
    grad_pieces = gather(grad)
    returned = lax.all_to_all(slots.reshape(8, TILE, 256), "grp", 0, 0, tiled=True).reshape(1024, 256)
    parts = lax.all_to_all(partial.reshape(8, 32, 256), "grp", 0, 0, tiled=True)
    part = jnp.sum(parts, axis=0)
    for step in (1, 2, 4, 8, 16):
        part = part + lax.ppermute(part, "blk", [(i, i ^ step) for i in range(NX * NZ)])
    part = part * float(65536) ** -0.5
    grad_weight = lax.all_to_all(jnp.broadcast_to(part[None], (8, 32, 256)), "grp", 0, 0, tiled=True)
    grad_features = call(
        functools.partial(backward_kernel, len(grad_pieces)),
        [dense, sel, returned, weight] + grad_pieces,
        shape((256, 256), BF),
        name="backward",
        flops=2 * 256 * 8192 * 256,
    )
    return hidden[None], grad_features[None], grad_weight.reshape(256, 256)


def solution(mesh):
    three, four = P("grp", "blk", None), P("grp", "blk", None, None)
    five = P("grp", "blk", None, None, None)
    return jax.shard_map(
        body,
        mesh=mesh,
        in_specs=(three, P(), three, five, three, five, three, three, four, three),
        out_specs=(three, three, P()),
        check_vma=False,
    )
```

time: 614 us -> 183 us (0.30)
  waiting for transfers between devices: 504 us -> 39 us
  starting transfers between devices: 14.2 us -> 92.8 us
  matrix products: 28.2 us -> 0 us
  other arithmetic: 16.4 us -> 1.13 us
  between operations: 13.9 us -> 1.05 us
  Pallas kernels: 0 us -> 12.5 us
    psum x1 -> x0, waiting for transfers between devices: 249 us -> none  [body(): lax.psum(partial_weight, ('blk', 'grp')) * float(vertex_total) ** (-0.5)]
    reduce_scatter x1 -> x0, waiting for transfers between devices: 184 us -> none  [body(): lax.psum_scatter(jnp.stack(pieces, axis=1).reshape(row_count * lax.axis_s...]
    ppermute x0 -> x53, starting transfers between devices: none -> 58.5 us  [the longest x32 32.7 us: go_z(): return lax.ppermute(v, 'blk', swap_z(kind))]
    all_gather x1 -> x0, waiting for transfers between devices: 46.9 us -> none  [body(): shards = lax.all_gather(projected, 'blk', axis=0, tiled=True)]
    ppermute x0 -> x53, waiting for transfers between devices: none -> 33.8 us  [the longest x32 19.3 us: go_z(): return lax.ppermute(v, 'blk', swap_z(kind))]
    dot_general x9 -> x0, matrix products: 28.2 us -> none  [the longest x1 4.58 us: body(): jnp.einsum('uij,ujh->uih', sparse_vals, received[col_block], preferred_el...]
    unnamed x19 -> x104, local copies, waits for them, and re-layouts: 0.88 us -> 28.9 us
    all_to_all x2 -> x4, starting transfers between devices: 14.2 us -> 34.3 us  [the longest x1 12.2 us: body(): lax.all_to_all(outgoing, 'grp', 0, 0, tiled=True).reshape(1024, 256)]
  transfers between devices with their start and end apart: 5 -> 57, of which waited for: 5 -> 18; matrix products, arithmetic and copies ran while one was open for 7% -> 4% of each run, Pallas kernels for 0% -> 3%
where the time goes in v1:
time: 183 us; the launch traced here: 182 us
  starting transfers between devices  92.8 us (51%)
  waiting for transfers between devices  39 us (21%)
  local copies, waits for them, and re-layouts  35 us (19%)
  Pallas kernels  12.5 us (7%)
    ppermute x32, starting transfers between devices, go_z(): return lax.ppermute(v, 'blk', swap_z(kind))  32.7 us
    unnamed x104, local copies, waits for them, and re-layouts  28.9 us
    ppermute x16, starting transfers between devices, go_x(): return lax.ppermute(v, 'blk', swap_x(kind))  19.5 us
    ppermute x32, waiting for transfers between devices, go_z(): return lax.ppermute(v, 'blk', swap_z(kind))  19.3 us
    pallas_call x5, Pallas kernels, call(): pl.pallas_call(kernel, out_shape=outs, in_specs=[SMEM] * scalars + [VMEM]...  12.5 us
    all_to_all x1, starting transfers between devices, body(): lax.all_to_all(outgoing, 'grp', 0, 0, tiled=True).reshape(1024, 256)  12.2 us
    all_to_all x1, starting transfers between devices, body(): lax.all_to_all(jnp.broadcast_to(part[None], (8, 32, 256)), 'grp', 0, 0, t...  11.4 us
    ppermute x5, waiting for transfers between devices, body(): lax.ppermute(part, 'blk', [(i, i ^ step) for i in range(NX * NZ)])  9.31 us
  transfers between devices with their start and end apart: 57, of which 18 were waited for; matrix products, arithmetic and copies ran while one was open for 4% of the time, Pallas kernels for 3%

profile of v1, /device:TPU:1, one launch (start us, length us, event | category | flops | bytes accessed | tf_op | source)
XLA Modules:
  0.0 181.6 jit_solution(5077010531986260169)
XLA Ops:
  1.6 6.5 %collective-permute-start.13 = (bf16[128,256]{1,0:T(8,128)(2,1)S(1)}, bf16[128,256]{1,0:T(8,128)(2,1)S(1)}, u32[]{:S(2)}, u32[]{:S(2)}) collective-permute-start(bf16[128,256]{1,0:T(8,128)(2,1)S(1)} %get-tuple-element.19), channel_id=1, source_target_pairs={{0,56},{8,16},{16,8},{24,32},{32,24},{40,48},{48,40},{56,0},{64,12... | collective-permute-start | bytes 196616 | tf_op jit(solution)/shard_map/ppermute | solution.py:36
  8.1 2.5 %collective-permute-start.1 = (bf16[128,256]{1,0:T(8,128)(2,1)S(1)}, bf16[128,256]{1,0:T(8,128)(2,1)S(1)}, u32[]{:S(2)}, u32[]{:S(2)}) collective-permute-start(bf16[128,256]{1,0:T(8,128)(2,1)S(1)} %get-tuple-element.20), channel_id=1, source_target_pairs={{0,192},{8,200},{16,208},{24,216},{32,224},{40,232},{48,240},{56,2... | collective-permute-start | bytes 196616 | tf_op jit(solution)/shard_map/ppermute | solution.py:40
  21.6 4.5 %collective-permute-done.17 = bf16[128,256]{1,0:T(8,128)(2,1)S(1)} collective-permute-done((bf16[128,256]{1,0:T(8,128)(2,1)S(1)}, bf16[128,256]{1,0:T(8,128)(2,1)S(1)}, u32[]{:S(2)}, u32[]{:S(2)}) %collective-permute-start.17) | collective-permute-done | bytes 65568 | tf_op jit(solution)/shard_map/ppermute | solution.py:36
  27.4 2.3 %collective-permute-done.18 = bf16[64,256]{1,0:T(8,128)(2,1)S(1)} collective-permute-done((bf16[64,256]{1,0:T(8,128)(2,1)S(1)}, bf16[64,256]{1,0:T(8,128)(2,1)S(1)}, u32[]{:S(2)}, u32[]{:S(2)}) %collective-permute-start.18) | collective-permute-done | bytes 32800 | tf_op jit(solution)/shard_map/ppermute | solution.py:36
  44.3 12.2 %all-to-all-start = ((bf16[8,128,256]{2,1,0:T(8,128)(2,1)}), bf16[8,128,256]{2,1,0:T(8,128)(2,1)S(1)}, u32[]{:S(2)}, u32[]{:S(2)}) async-start(bf16[8,128,256]{2,1,0:T(8,128)(2,1)} %get-tuple-element.9), calls=%async_computation | async-start | bytes 1048576 | tf_op jit(solution)/shard_map/all_to_all | solution.py:195
  59.9 2.1 %collective-permute-start.23 = (bf16[512,256]{1,0:T(8,128)(2,1)}, bf16[512,256]{1,0:T(8,128)(2,1)}, u32[]{:S(2)}, u32[]{:S(2)}) collective-permute-start(bf16[512,256]{1,0:T(8,128)(2,1)} %slice.95), channel_id=1, source_target_pairs={{0,192},{8,200},{16,208},{24,216},{32,224},{40,232},{48,240},{56,2... | collective-permute-start | bytes 786440 | tf_op jit(solution)/shard_map/ppermute | solution.py:40
  72.4 2.0 %copy-done = bf16[256,8192]{1,0:T(8,128)(2,1)} copy-done((bf16[256,8192]{1,0:T(8,128)(2,1)}, bf16[256,8192]{1,0:T(8,128)(2,1)S(1)}, u32[]{:S(2)}) %copy-start) | copy-done | bytes 4194328
  75.5 2.2 %copy-done.1 = bf16[256,8192]{1,0:T(8,128)(2,1)S(1)} copy-done((bf16[256,8192]{1,0:T(8,128)(2,1)S(1)}, bf16[256,8192]{1,0:T(8,128)(2,1)}, u32[]{:S(2)}) %copy-start.1) | copy-done | bytes 4194328
  85.2 4.5 %forward.1 = (bf16[256,256]{1,0:T(8,128)(2,1)}, bf16[256,256]{1,0:T(8,128)(2,1)S(1)}, bf16[1024,256]{1,0:T(8,128)(2,1)S(1)}, f32[256,256]{1,0:T(8,128)S(1)}) custom-call(bf16[256,8192]{1,0:T(8,128)(2,1)S(1)} %copy-done.1, bf16[256,2048]{1,0:T(8,128)(2,1)S(1)} %sparse.1.refs_1_, bf16[1024,256]{1,0:T(8,128)(2,1)S(1)} %bitcast.26, ...), custom_call_target="tpu_custom_call" | custom-call | flops 1073741824 | bytes 11272192 | tf_op jit(solution)/shard_map/forward/pallas_call | solution.py:159
  92.4 6.3 %all-to-all-start.2 = ((f32[8,32,256]{2,1,0:T(8,128)}), f32[8,32,256]{2,1,0:T(8,128)S(1)}, u32[]{:S(2)}, u32[]{:S(2)}) async-start(f32[8,32,256]{2,1,0:T(8,128)} %bitcast.32), calls=%async_computation.2 | async-start | bytes 524288 | tf_op jit(solution)/shard_map/all_to_all | solution.py:221
  100.5 2.5 %collective-permute-start.27 = (bf16[64,256]{1,0:T(8,128)(2,1)S(1)}, bf16[64,256]{1,0:T(8,128)(2,1)S(1)}, u32[]{:S(2)}, u32[]{:S(2)}) collective-permute-start(bf16[64,256]{1,0:T(8,128)(2,1)S(1)} %slice.97), channel_id=1, source_target_pairs={{0,192},{8,200},{16,208},{24,216},{32,224},{40,232},{48,240},{56,2... | collective-permute-start | bytes 98312 | tf_op jit(solution)/shard_map/ppermute | solution.py:40
  107.7 2.1 %collective-permute-start.41 = (bf16[128,256]{1,0:T(8,128)(2,1)S(1)}, bf16[128,256]{1,0:T(8,128)(2,1)S(1)}, u32[]{:S(2)}, u32[]{:S(2)}) collective-permute-start(bf16[128,256]{1,0:T(8,128)(2,1)S(1)} %collective-permute-done.38), channel_id=1, source_target_pairs={{0,56},{8,16},{16,8},{24,32},{32,24},{40,48},{48,40},{56,0},{64,12... | collective-permute-start | bytes 196616 | tf_op jit(solution)/shard_map/ppermute | solution.py:36
  111.4 5.3 %collective-permute-done.41 = bf16[128,256]{1,0:T(8,128)(2,1)S(1)} collective-permute-done((bf16[128,256]{1,0:T(8,128)(2,1)S(1)}, bf16[128,256]{1,0:T(8,128)(2,1)S(1)}, u32[]{:S(2)}, u32[]{:S(2)}) %collective-permute-start.41) | collective-permute-done | bytes 65568 | tf_op jit(solution)/shard_map/ppermute | solution.py:36
  119.4 2.3 %collective-permute-done.49 = f32[32,256]{1,0:T(8,128)S(1)} collective-permute-done((f32[32,256]{1,0:T(8,128)S(1)}, f32[32,256]{1,0:T(8,128)S(1)}, u32[]{:S(2)}, u32[]{:S(2)}) %collective-permute-start.49) | collective-permute-done | bytes 32800 | tf_op jit(solution)/shard_map/ppermute | solution.py:224
  121.7 2.7 %collective-permute-start.50 = (f32[32,256]{1,0:T(8,128)S(1)}, f32[32,256]{1,0:T(8,128)S(1)}, u32[]{:S(2)}, u32[]{:S(2)}) collective-permute-start(f32[32,256]{1,0:T(8,128)S(1)} %add.22), channel_id=1, source_target_pairs={{0,32},{8,40},{16,48},{24,56},{32,0},{40,8},{48,16},{56,24},{64,96... | collective-permute-start | bytes 98312 | tf_op jit(solution)/shard_map/ppermute | solution.py:224
  124.5 3.9 %collective-permute-done.50 = f32[32,256]{1,0:T(8,128)S(1)} collective-permute-done((f32[32,256]{1,0:T(8,128)S(1)}, f32[32,256]{1,0:T(8,128)S(1)}, u32[]{:S(2)}, u32[]{:S(2)}) %collective-permute-start.50) | collective-permute-done | bytes 32800 | tf_op jit(solution)/shard_map/ppermute | solution.py:224
  128.4 3.0 %collective-permute-done.51 = f32[32,256]{1,0:T(8,128)S(1)} collective-permute-done((f32[32,256]{1,0:T(8,128)S(1)}, f32[32,256]{1,0:T(8,128)S(1)}, u32[]{:S(2)}, u32[]{:S(2)}) %collective-permute-start.51) | collective-permute-done | bytes 32800 | tf_op jit(solution)/shard_map/ppermute | solution.py:224
  137.0 11.4 %all-to-all-start.3 = ((f32[8,32,256]{2,1,0:T(8,128)}), f32[8,32,256]{2,1,0:T(8,128)S(1)}, u32[]{:S(2)}, u32[]{:S(2)}) async-start(f32[8,32,256]{2,1,0:T(8,128)} %broadcast_in_dim.14), calls=%async_computation.3 | async-start | bytes 524288 | tf_op jit(solution)/shard_map/all_to_all | solution.py:226
  149.8 5.1 %all-to-all-done.3 = f32[8,32,256]{2,1,0:T(8,128)S(1)} async-done(((f32[8,32,256]{2,1,0:T(8,128)}), f32[8,32,256]{2,1,0:T(8,128)S(1)}, u32[]{:S(2)}, u32[]{:S(2)}) %all-to-all-start.3) | async-done | bytes 262176 | tf_op jit(solution)/shard_map/all_to_all | solution.py:226
  155.5 4.4 %all-to-all-start.1 = ((bf16[8,128,256]{2,1,0:T(8,128)(2,1)}), bf16[8,128,256]{2,1,0:T(8,128)(2,1)S(1)}, u32[]{:S(2)}, u32[]{:S(2)}) async-start(bf16[8,128,256]{2,1,0:T(8,128)(2,1)} %bitcast.30), calls=%async_computation.1 | async-start | bytes 1048576 | tf_op jit(solution)/shard_map/all_to_all | solution.py:220
  165.0 3.1 %collective-permute-done.34 = bf16[256,256]{1,0:T(8,128)(2,1)S(1)} collective-permute-done((bf16[256,256]{1,0:T(8,128)(2,1)S(1)}, bf16[256,256]{1,0:T(8,128)(2,1)S(1)}, u32[]{:S(2)}, u32[]{:S(2)}) %collective-permute-start.34) | collective-permute-done | bytes 131104 | tf_op jit(solution)/shard_map/ppermute | solution.py:36
  169.5 2.0 %collective-permute-done.47.refs_16_ = bf16[512,256]{1,0:T(8,128)(2,1)} collective-permute-done((bf16[512,256]{1,0:T(8,128)(2,1)}, bf16[512,256]{1,0:T(8,128)(2,1)}, u32[]{:S(2)}, u32[]{:S(2)}) %collective-permute-start.47) | collective-permute-done | bytes 262176 | tf_op jit(solution)/shard_map/ppermute | solution.py:40
  171.5 2.2 %copy-done.2 = bf16[256,8192]{1,0:T(8,128)(2,1)S(1)} copy-done((bf16[256,8192]{1,0:T(8,128)(2,1)S(1)}, bf16[256,8192]{1,0:T(8,128)(2,1)}, u32[]{:S(2)}) %copy-start.2) | copy-done | bytes 4194328
  177.5 3.4 %backward.1 = bf16[256,256]{1,0:T(8,128)(2,1)} custom-call(bf16[256,8192]{1,0:T(8,128)(2,1)S(1)} %copy-done.2, bf16[256,1024]{1,0:T(8,128)(2,1)S(1)} %copy-done.11, bf16[1024,256]{1,0:T(8,128)(2,1)S(1)} %bitcast.27, bf16[256,256]{1,0:T(8,128)(2,1)S(1)} %copy-done.9, bf16[512,256]{1,0:T(8,128)(2,1)S(1)} %copy-done.15, bf16[512,256]{1,0:T(8,128)(2,1)S(1)} %copy-done.21, ...), custom_call_target="tpu_custom_call" | custom-call | flops 1073741824 | bytes 9699328 | tf_op jit(solution)/shard_map/backward/pallas_call | solution.py:159
  (231 shorter events, 82.0 us)
Async XLA Ops:
  1.6 13.4 %collective-permute-start.13 = (bf16[128,256]{1,0:T(8,128)(2,1)S(1)}, bf16[128,256]{1,0:T(8,128)(2,1)S(1)}, u32[]{:S(2)}, u32[]{:S(2)}) collective-permute-start(bf16[128,256]{1,0:T(8,128)(2,1)S(1)} %get-tuple-element.19), channel_id=1, source_target_pairs={{0,56},{8,16},{16,8},{24,32},{32,24},{40,48},{48,40},{56,0},{64,12... | collective-permute-start | bytes 196616 | tf_op jit(solution)/shard_map/ppermute | solution.py:36
  17.9 13.6 %collective-permute-start.5 = (bf16[512,256]{1,0:T(8,128)(2,1)S(1)}, bf16[512,256]{1,0:T(8,128)(2,1)S(1)}, u32[]{:S(2)}, u32[]{:S(2)}) collective-permute-start(bf16[512,256]{1,0:T(8,128)(2,1)S(1)} %constant_dynamic-update-slice_fusion.refs_5_), channel_id=1, source_target_pairs={{0,56},{8,16},{16,8},{24,32},{32,24},{40,48},{48,40},{56,0},{64,12... | collective-permute-start | bytes 786440 | tf_op jit(solution)/shard_map/ppermute | solution.py:36
  19.4 13.0 %collective-permute-start.4 = (bf16[512,256]{1,0:T(8,128)(2,1)S(1)}, bf16[512,256]{1,0:T(8,128)(2,1)S(1)}, u32[]{:S(2)}, u32[]{:S(2)}) collective-permute-start(bf16[512,256]{1,0:T(8,128)(2,1)S(1)} %constant_dynamic-update-slice_fusion.refs_5_), channel_id=1, source_target_pairs={{0,8},{8,0},{16,24},{24,16},{32,40},{40,32},{48,56},{56,48},{64,72... | collective-permute-start | bytes 786440 | tf_op jit(solution)/shard_map/ppermute | solution.py:36
  30.3 26.3 %collective-permute-start.21 = (bf16[1024,256]{1,0:T(8,128)(2,1)S(1)}, bf16[1024,256]{1,0:T(8,128)(2,1)S(1)}, u32[]{:S(2)}, u32[]{:S(2)}) collective-permute-start(bf16[1024,256]{1,0:T(8,128)(2,1)S(1)} %constant_dynamic-update-slice_fusion.5.refs_13_), channel_id=1, source_target_pairs={{0,192},{8,200},{16,208},{24,216},{32,224},{40,232},{48,240},{56,2... | collective-permute-start | bytes 1572872 | tf_op jit(solution)/shard_map/ppermute | solution.py:40
  31.5 27.7 %collective-permute-start.20 = (bf16[1024,256]{1,0:T(8,128)(2,1)S(1)}, bf16[1024,256]{1,0:T(8,128)(2,1)S(1)}, u32[]{:S(2)}, u32[]{:S(2)}) collective-permute-start(bf16[1024,256]{1,0:T(8,128)(2,1)S(1)} %constant_dynamic-update-slice_fusion.5.refs_13_), channel_id=1, source_target_pairs={{0,64},{8,72},{16,80},{24,88},{32,96},{40,104},{48,112},{56,120},{... | collective-permute-start | bytes 1572872 | tf_op jit(solution)/shard_map/ppermute | solution.py:40
  36.7 25.4 %collective-permute-start.9 = (bf16[512,256]{1,0:T(8,128)(2,1)S(1)}, bf16[512,256]{1,0:T(8,128)(2,1)S(1)}, u32[]{:S(2)}, u32[]{:S(2)}) collective-permute-start(bf16[512,256]{1,0:T(8,128)(2,1)S(1)} %collective-permute-done.6.refs_8_), channel_id=1, source_target_pairs={{0,56},{8,16},{16,8},{24,32},{32,24},{40,48},{48,40},{56,0},{64,12... | collective-permute-start | bytes 786440 | tf_op jit(solution)/shard_map/ppermute | solution.py:36
  38.8 25.8 %collective-permute-start.8 = (bf16[512,256]{1,0:T(8,128)(2,1)S(1)}, bf16[512,256]{1,0:T(8,128)(2,1)S(1)}, u32[]{:S(2)}, u32[]{:S(2)}) collective-permute-start(bf16[512,256]{1,0:T(8,128)(2,1)S(1)} %collective-permute-done.7.refs_9_), channel_id=1, source_target_pairs={{0,8},{8,0},{16,24},{24,16},{32,40},{40,32},{48,56},{56,48},{64,72... | collective-permute-start | bytes 786440 | tf_op jit(solution)/shard_map/ppermute | solution.py:36
  44.3 31.1 %all-to-all-start = ((bf16[8,128,256]{2,1,0:T(8,128)(2,1)}), bf16[8,128,256]{2,1,0:T(8,128)(2,1)S(1)}, u32[]{:S(2)}, u32[]{:S(2)}) async-start(bf16[8,128,256]{2,1,0:T(8,128)(2,1)} %get-tuple-element.9), calls=%async_computation | async-start | bytes 1048576 | tf_op jit(solution)/shard_map/all_to_all | solution.py:195
  57.3 18.1 %collective-permute-start.22 = (bf16[512,256]{1,0:T(8,128)(2,1)}, bf16[512,256]{1,0:T(8,128)(2,1)}, u32[]{:S(2)}, u32[]{:S(2)}) collective-permute-start(bf16[512,256]{1,0:T(8,128)(2,1)} %slice.94), channel_id=1, source_target_pairs={{0,64},{8,72},{16,80},{24,88},{32,96},{40,104},{48,112},{56,120},{... | collective-permute-start | bytes 786440 | tf_op jit(solution)/shard_map/ppermute | solution.py:40
  59.9 15.5 %collective-permute-start.23 = (bf16[512,256]{1,0:T(8,128)(2,1)}, bf16[512,256]{1,0:T(8,128)(2,1)}, u32[]{:S(2)}, u32[]{:S(2)}) collective-permute-start(bf16[512,256]{1,0:T(8,128)(2,1)} %slice.95), channel_id=1, source_target_pairs={{0,192},{8,200},{16,208},{24,216},{32,224},{40,232},{48,240},{56,2... | collective-permute-start | bytes 786440 | tf_op jit(solution)/shard_map/ppermute | solution.py:40
  92.4 12.4 %collective-permute-start.36 = (bf16[128,256]{1,0:T(8,128)(2,1)S(1)}, bf16[128,256]{1,0:T(8,128)(2,1)S(1)}, u32[]{:S(2)}, u32[]{:S(2)}) collective-permute-start(bf16[128,256]{1,0:T(8,128)(2,1)S(1)} %get-tuple-element.15), channel_id=1, source_target_pairs={{0,8},{8,0},{16,24},{24,16},{32,40},{40,32},{48,56},{56,48},{64,72... | collective-permute-start | bytes 196616 | tf_op jit(solution)/shard_map/ppermute | solution.py:36
  92.4 17.5 %all-to-all-start.2 = ((f32[8,32,256]{2,1,0:T(8,128)}), f32[8,32,256]{2,1,0:T(8,128)S(1)}, u32[]{:S(2)}, u32[]{:S(2)}) async-start(f32[8,32,256]{2,1,0:T(8,128)} %bitcast.32), calls=%async_computation.2 | async-start | bytes 524288 | tf_op jit(solution)/shard_map/all_to_all | solution.py:221
  106.2 28.0 %collective-permute-start.29 = (bf16[512,256]{1,0:T(8,128)(2,1)S(1)}, bf16[512,256]{1,0:T(8,128)(2,1)S(1)}, u32[]{:S(2)}, u32[]{:S(2)}) collective-permute-start(bf16[512,256]{1,0:T(8,128)(2,1)S(1)} %constant_dynamic-update-slice_fusion.14.refs_4_), channel_id=1, source_target_pairs={{0,56},{8,16},{16,8},{24,32},{32,24},{40,48},{48,40},{56,0},{64,12... | collective-permute-start | bytes 786440 | tf_op jit(solution)/shard_map/ppermute | solution.py:36
  107.7 27.3 %collective-permute-start.28 = (bf16[512,256]{1,0:T(8,128)(2,1)S(1)}, bf16[512,256]{1,0:T(8,128)(2,1)S(1)}, u32[]{:S(2)}, u32[]{:S(2)}) collective-permute-start(bf16[512,256]{1,0:T(8,128)(2,1)S(1)} %constant_dynamic-update-slice_fusion.14.refs_4_), channel_id=1, source_target_pairs={{0,8},{8,0},{16,24},{24,16},{32,40},{40,32},{48,56},{56,48},{64,72... | collective-permute-start | bytes 786440 | tf_op jit(solution)/shard_map/ppermute | solution.py:36
  116.6 11.8 %collective-permute-start.42 = (bf16[64,256]{1,0:T(8,128)(2,1)S(1)}, bf16[64,256]{1,0:T(8,128)(2,1)S(1)}, u32[]{:S(2)}, u32[]{:S(2)}) collective-permute-start(bf16[64,256]{1,0:T(8,128)(2,1)S(1)} %slice.100), channel_id=1, source_target_pairs={{0,8},{8,0},{16,24},{24,16},{32,40},{40,32},{48,56},{56,48},{64,72... | collective-permute-start | bytes 98312 | tf_op jit(solution)/shard_map/ppermute | solution.py:36
  116.7 15.5 %collective-permute-start.43 = (bf16[64,256]{1,0:T(8,128)(2,1)S(1)}, bf16[64,256]{1,0:T(8,128)(2,1)S(1)}, u32[]{:S(2)}, u32[]{:S(2)}) collective-permute-start(bf16[64,256]{1,0:T(8,128)(2,1)S(1)} %slice.101), channel_id=1, source_target_pairs={{0,56},{8,16},{16,8},{24,32},{32,24},{40,48},{48,40},{56,0},{64,12... | collective-permute-start | bytes 98312 | tf_op jit(solution)/shard_map/ppermute | solution.py:36
  132.2 27.8 %collective-permute-start.45 = (bf16[1024,256]{1,0:T(8,128)(2,1)S(1)}, bf16[1024,256]{1,0:T(8,128)(2,1)S(1)}, u32[]{:S(2)}, u32[]{:S(2)}) collective-permute-start(bf16[1024,256]{1,0:T(8,128)(2,1)S(1)} %constant_dynamic-update-slice_fusion.19.refs_12_), channel_id=1, source_target_pairs={{0,192},{8,200},{16,208},{24,216},{32,224},{40,232},{48,240},{56,2... | collective-permute-start | bytes 1572872 | tf_op jit(solution)/shard_map/ppermute | solution.py:40
  133.9 27.8 %collective-permute-start.44 = (bf16[1024,256]{1,0:T(8,128)(2,1)S(1)}, bf16[1024,256]{1,0:T(8,128)(2,1)S(1)}, u32[]{:S(2)}, u32[]{:S(2)}) collective-permute-start(bf16[1024,256]{1,0:T(8,128)(2,1)S(1)} %constant_dynamic-update-slice_fusion.19.refs_12_), channel_id=1, source_target_pairs={{0,64},{8,72},{16,80},{24,88},{32,96},{40,104},{48,112},{56,120},{... | collective-permute-start | bytes 1572872 | tf_op jit(solution)/shard_map/ppermute | solution.py:40
  134.1 14.2 %collective-permute-start.30 = (bf16[512,256]{1,0:T(8,128)(2,1)S(1)}, bf16[512,256]{1,0:T(8,128)(2,1)S(1)}, u32[]{:S(2)}, u32[]{:S(2)}) collective-permute-start(bf16[512,256]{1,0:T(8,128)(2,1)S(1)} %collective-permute-done.29.refs_6_), channel_id=1, source_target_pairs={{0,8},{8,0},{16,24},{24,16},{32,40},{40,32},{48,56},{56,48},{64,72... | collective-permute-start | bytes 786440 | tf_op jit(solution)/shard_map/ppermute | solution.py:36
  134.9 14.8 %collective-permute-start.31 = (bf16[512,256]{1,0:T(8,128)(2,1)S(1)}, bf16[512,256]{1,0:T(8,128)(2,1)}, u32[]{:S(2)}, u32[]{:S(2)}) collective-permute-start(bf16[512,256]{1,0:T(8,128)(2,1)S(1)} %collective-permute-done.28.refs_5_), channel_id=1, source_target_pairs={{0,56},{8,16},{16,8},{24,32},{32,24},{40,48},{48,40},{56,0},{64,12... | collective-permute-start | bytes 786440 | tf_op jit(solution)/shard_map/ppermute | solution.py:36
  137.0 17.9 %all-to-all-start.3 = ((f32[8,32,256]{2,1,0:T(8,128)}), f32[8,32,256]{2,1,0:T(8,128)S(1)}, u32[]{:S(2)}, u32[]{:S(2)}) async-start(f32[8,32,256]{2,1,0:T(8,128)} %broadcast_in_dim.14), calls=%async_computation.3 | async-start | bytes 524288 | tf_op jit(solution)/shard_map/all_to_all | solution.py:226
  148.4 15.1 %collective-permute-start.33 = (bf16[512,256]{1,0:T(8,128)(2,1)S(1)}, bf16[512,256]{1,0:T(8,128)(2,1)S(1)}, u32[]{:S(2)}, u32[]{:S(2)}) collective-permute-start(bf16[512,256]{1,0:T(8,128)(2,1)S(1)} %collective-permute-done.30.refs_7_), channel_id=1, source_target_pairs={{0,56},{8,16},{16,8},{24,32},{32,24},{40,48},{48,40},{56,0},{64,12... | collective-permute-start | bytes 786440 | tf_op jit(solution)/shard_map/ppermute | solution.py:36
  149.8 14.0 %collective-permute-start.32 = (bf16[512,256]{1,0:T(8,128)(2,1)}, bf16[512,256]{1,0:T(8,128)(2,1)S(1)}, u32[]{:S(2)}, u32[]{:S(2)}) collective-permute-start(bf16[512,256]{1,0:T(8,128)(2,1)} %collective-permute-done.31.refs_8_), channel_id=1, source_target_pairs={{0,8},{8,0},{16,24},{24,16},{32,40},{40,32},{48,56},{56,48},{64,72... | collective-permute-start | bytes 786440 | tf_op jit(solution)/shard_map/ppermute | solution.py:36
  155.5 13.9 %all-to-all-start.1 = ((bf16[8,128,256]{2,1,0:T(8,128)(2,1)}), bf16[8,128,256]{2,1,0:T(8,128)(2,1)S(1)}, u32[]{:S(2)}, u32[]{:S(2)}) async-start(bf16[8,128,256]{2,1,0:T(8,128)(2,1)} %bitcast.30), calls=%async_computation.1 | async-start | bytes 1048576 | tf_op jit(solution)/shard_map/all_to_all | solution.py:220
  (74 other events, 687.7 us)

commit v2 on v1

v2 whole, which is shorter than its diff:
```python
import jax
import jax.numpy as jnp
from jax import lax
from jax.experimental import pallas as pl
from jax.experimental.pallas import tpu as pltpu
from jax.sharding import PartitionSpec as P

NX, NZ = 4, 8
TILE = 128
PIECES = 12
SELECT_AT = 1
BF = jnp.bfloat16
F32 = jnp.float32
VMEM_LIMIT = 58 * 1024 * 1024


def swap_z(kind):
    def partner(z):
        if kind == 0:
            return z ^ 1
        return (z - 1) % NZ if z % 2 == 0 else (z + 1) % NZ

    return [(x * NZ + z, x * NZ + partner(z)) for x in range(NX) for z in range(NZ)]


def swap_x(kind):
    def partner(x):
        if kind == 0:
            return x ^ 1
        return (x - 1) % NX if x % 2 == 0 else (x + 1) % NX

    return [(x * NZ + z, partner(x) * NZ + z) for x in range(NX) for z in range(NZ)]


def go_z(v, kind):
    return lax.ppermute(v, "blk", swap_z(kind))


def go_x(v, kind):
    return lax.ppermute(v, "blk", swap_x(kind))


def across_z(v):
    return lax.ppermute(v, "blk", [(i, i ^ 4) for i in range(NX * NZ)])


def tie(values, *others):
    return lax.optimization_barrier((values, others))[0]


def gather(v, hook):
    u1, d1, across = go_z(v, 0), go_z(v, 1), across_z(v)
    u1, d1 = hook(0, (u1, d1))
    u2, d2 = go_z(d1, 0), go_z(u1, 1)
    p = jnp.concatenate([v, u1, d1])
    pu, pd = go_x(p, 0), go_x(p, 1)
    u2, d2 = hook(1, (u2, d2))
    u3, d3 = go_z(d2, 0), go_z(u2, 1)
    q = jnp.concatenate([u2, d2, across])
    qu, qd = go_x(q, 0), go_x(q, 1)
    u3, d3 = hook(2, (u3, d3))
    r = jnp.concatenate([u3, d3])
    ru, rd = go_x(r, 0), go_x(r, 1)
    pu, pd = hook(3, (pu, pd))
    px = go_x(tie(pd, pu), 0)
    qu, qd = hook(4, (qu, qd))
    qx = go_x(tie(qu, qd), 1)
    ru, rd = hook(5, (ru, rd))
    rx = go_x(tie(rd, ru), 0)
    hook(6, px)
    return [p, pu, pd, px, q, qu, qd, qx, r, ru, rd, rx]


def dot(a, b, ca=1, cb=0):
    return lax.dot_general(a, b, (((ca,), (cb,)), ((), ())), preferred_element_type=F32)


def load(pairs, sems):
    copies = [pltpu.make_async_copy(src, dst, sems.at[i]) for i, (src, dst) in enumerate(pairs)]
    for c in copies:
        c.start()
    return copies


def select_kernel(count_any, rows_any, x_any, sel_ref, out_ref, count_ref, rows_ref, x_ref, sems):
    for c in load([(count_any, count_ref), (rows_any, rows_ref), (x_any, x_ref)], sems):
        c.wait()
    lane = lax.broadcasted_iota(jnp.int32, (1, TILE), 1)
    row = lax.broadcasted_iota(jnp.int32, (2 * TILE, TILE), 0)
    for s in range(8):
        listed = jnp.where(lane < count_ref[s], rows_ref[s : s + 1, :], -1)
        sel = jnp.where(row == listed, 1.0, 0.0).astype(BF)
        sel_ref[:, s * TILE : (s + 1) * TILE] = sel
        out_ref[s] = dot(sel, x_ref[...], 0, 0).astype(BF)


def sparse_kernel(rows_any, cols_any, tiles_any, rec_any, out_ref, sum_ref, rows_ref, cols_ref, tiles_ref, rec_ref, total, sems):
    copies = load([(rows_any, rows_ref), (cols_any, cols_ref), (tiles_any, tiles_ref), (rec_any, rec_ref)], sems)
    total[...] = jnp.zeros_like(total)
    for c in copies:
        c.wait()
    for u in range(32):
        at = rows_ref[u] * 8 + cols_ref[u]
        total[at] += tiles_ref[u].astype(F32)
    for r in range(2):
        rows = slice(r * TILE, (r + 1) * TILE)
        for q in range(8):
            high, low = split(total[r * 8 + q])
            out_ref[rows, q * TILE : (q + 1) * TILE] = high
            out_ref[rows, (8 + q) * TILE : (9 + q) * TILE] = low
    half = 8 * TILE
    sum_ref[...] = dot(out_ref[:, :half], rec_ref[...]) + dot(out_ref[:, half:], rec_ref[...])


def split(v):
    high = v.astype(BF)
    return high, (v - high.astype(F32)).astype(BF)


def dense_product(cols_ref, tiles_ref, piece_any, pieces, sems, ready):
    copies = load(list(zip(piece_any, pieces)), sems)
    for c in ready:
        c.wait()
    blk = lax.axis_index("blk")
    x, z = blk // NZ, blk % NZ
    sx, sz = 1 - 2 * (x % 2), 1 - 2 * (z % 2)
    xs = [lax.rem(x + NX + k * sx, NX) * NZ for k in (0, 1, -1, 2)]
    zs = [[lax.rem(z + NZ + k * sz, NZ) for k in part] for part in ((0, 1, -1), (2, -2, 4), (3, -3))]
    sums = [jnp.zeros((TILE, 2 * TILE), F32) for _ in range(2)]
    held = []
    for i, part in enumerate(zs):
        for j, xv in enumerate(xs):
            held += [(xv + zv, 4 * i + j, 2 * TILE * k) for k, zv in enumerate(part)]
    waited = set()
    for n in range(0, len(held), 2):
        pair = held[n : n + 2]
        for _, piece, _ in pair:
            if piece not in waited:
                copies[piece].wait()
                waited.add(piece)
        for r in range(2):
            left = jnp.concatenate([tiles_ref[2 * c + r] for c, _, _ in pair], axis=1)
            right = [
                pieces[p][pl.ds(pl.multiple_of(at + cols_ref[2 * c + r] * TILE, TILE), TILE), :] for c, p, at in pair
            ]
            sums[r] = sums[r] + dot(left, jnp.concatenate(right, axis=0))
    return jnp.concatenate(sums, axis=0)


def forward_kernel(*refs):
    cols_any, tiles_any, s_any, sum_any, w_any, cot_any = refs[:6]
    pieces = refs[6 : 6 + PIECES]
    hidden_ref, grad_ref, back_ref = refs[6 + PIECES : 9 + PIECES]
    cols_ref, tiles_ref, s_ref, sum_ref, w_ref, cot_ref, sems, piece_sems = refs[9 + PIECES : 16 + PIECES + 1]
    ins = [(cols_any, cols_ref), (tiles_any, tiles_ref), (sum_any, sum_ref)]
    copies = load(ins + [(w_any, w_ref), (cot_any, cot_ref), (s_any, s_ref)], sems)
    agg = dense_product(cols_ref, tiles_ref, pieces, refs[-PIECES:], piece_sems, copies[:2])
    for c in copies[2:]:
        c.wait()
    half = 8 * TILE
    high, low = split(agg + sum_ref[...])
    pre = dot(high, w_ref[...]) + dot(low, w_ref[...])
    sig = jax.nn.sigmoid(pre)
    hidden_ref[...] = (pre * sig).astype(BF)
    grad = (cot_ref[...].astype(F32) * sig * (1.0 + pre * (1.0 - sig))).astype(BF)
    grad_ref[...] = grad
    slots = (dot(s_ref[:, :half], grad, 0, 0) + dot(s_ref[:, half:], grad, 0, 0)).astype(BF)
    high, low = split(dot(high, grad, 0, 0) + dot(low, grad, 0, 0))
    for g in range(8):
        back_ref[g, :TILE] = slots[g * TILE : (g + 1) * TILE]
        back_ref[g, TILE : TILE + 32] = high[g * 32 : (g + 1) * 32]
        back_ref[g, TILE + 32 :] = low[g * 32 : (g + 1) * 32]


def backward_kernel(*refs):
    cols_any, tiles_any, sel_any, ret_any, w_any = refs[:5]
    pieces = refs[5 : 5 + PIECES]
    out_ref, cols_ref, tiles_ref, sel_ref, ret_ref, w_ref, sems, piece_sems = refs[5 + PIECES : 13 + PIECES]
    ins = [(cols_any, cols_ref), (tiles_any, tiles_ref), (sel_any, sel_ref)]
    copies = load(ins + [(ret_any, ret_ref), (w_any, w_ref)], sems)
    agg = dense_product(cols_ref, tiles_ref, pieces, refs[-PIECES:], piece_sems, copies[:2])
    for c in copies[2:]:
        c.wait()
    for g in range(8):
        agg += dot(sel_ref[:, g * TILE : (g + 1) * TILE], ret_ref[g, :TILE])
    out_ref[...] = dot(agg.astype(BF), w_ref[...], 1, 1).astype(BF)


HBM = pl.BlockSpec(memory_space=pltpu.HBM)
VMEM = pl.BlockSpec(memory_space=pltpu.VMEM)
DMA = pltpu.SemaphoreType.DMA


def call(kernel, ins, outs, scratch, name, flops, pieces=()):
    many = isinstance(outs, list)
    moved = sum(v.size * v.dtype.itemsize for v in list(ins) + (outs if many else [outs]))
    return pl.pallas_call(
        kernel,
        out_shape=outs,
        in_specs=[HBM] * (len(ins) + len(pieces)),
        out_specs=[VMEM] * len(outs) if many else VMEM,
        scratch_shapes=scratch + [pltpu.VMEM(p.shape, BF) for p in pieces],
        compiler_params=pltpu.CompilerParams(vmem_limit_bytes=VMEM_LIMIT),
        cost_estimate=pl.CostEstimate(flops=flops, bytes_accessed=moved, transcendentals=0),
        name=name,
    )(*ins, *pieces)


def body(
    features,
    weight,
    cotangent,
    dense_tiles,
    dense_cols,
    sparse_tiles,
    sparse_rows,
    sparse_cols,
    send_rows,
    send_counts,
):
    shape = jax.ShapeDtypeStruct
    own = features[0]
    ints, tiles = dense_cols[0, 0], dense_tiles[0, 0]
    square = (256, 256)
    held = []
    for i, part in enumerate(zs):
        for j, xv in enumerate(xs):
            held += [(xv + zv, pieces[4 * i + j], 2 * TILE * k) for k, zv in enumerate(part)]
    for n in range(0, len(held), 2):
        pair = held[n : n + 2]
        for r in range(2):
            left = jnp.concatenate([tiles_ref[2 * c + r] for c, _, _ in pair], axis=1)
            right = [ref[pl.ds(pl.multiple_of(at + cols_ref[2 * c + r] * TILE, TILE), TILE), :] for c, ref, at in pair]
            sums[r] = sums[r] + dot(left, jnp.concatenate(right, axis=0))
    return jnp.concatenate(sums, axis=0)


def forward_kernel(*refs):
    cols_any, tiles_any, s_any, sum_any, w_any, cot_any = refs[:6]
    pieces = refs[6 : 6 + PIECES]
    hidden_ref, grad_ref, back_ref = refs[6 + PIECES : 9 + PIECES]
    cols_ref, tiles_ref, s_ref, sum_ref, w_ref, cot_ref, sems, piece_sems = refs[9 + PIECES : 16 + PIECES + 1]
    ins = [(cols_any, cols_ref), (tiles_any, tiles_ref), (sum_any, sum_ref)]
    copies = load(ins + [(w_any, w_ref), (cot_any, cot_ref), (s_any, s_ref)], sems)
    agg = dense_product(cols_ref, tiles_ref, pieces, refs[-PIECES:], piece_sems, copies[:2])
    for c in copies[2:]:
        c.wait()
    half = 8 * TILE
    high, low = split(agg + sum_ref[...])
    pre = dot(high, w_ref[...]) + dot(low, w_ref[...])
    sig = jax.nn.sigmoid(pre)
    hidden_ref[...] = (pre * sig).astype(BF)
    grad = (cot_ref[...].astype(F32) * sig * (1.0 + pre * (1.0 - sig))).astype(BF)
    grad_ref[...] = grad
    slots = (dot(s_ref[:, :half], grad, 0, 0) + dot(s_ref[:, half:], grad, 0, 0)).astype(BF)
    high, low = split(dot(high, grad, 0, 0) + dot(low, grad, 0, 0))
    for g in range(8):
        back_ref[g, :TILE] = slots[g * TILE : (g + 1) * TILE]
        back_ref[g, TILE : TILE + 32] = high[g * 32 : (g + 1) * 32]
        back_ref[g, TILE + 32 :] = low[g * 32 : (g + 1) * 32]


def backward_kernel(*refs):
    cols_any, tiles_any, sel_any, ret_any, w_any = refs[:5]
    pieces = refs[5 : 5 + PIECES]
    out_ref, cols_ref, tiles_ref, sel_ref, ret_ref, w_ref, sems, piece_sems = refs[5 + PIECES : 13 + PIECES]
    ins = [(cols_any, cols_ref), (tiles_any, tiles_ref), (sel_any, sel_ref)]
    copies = load(ins + [(ret_any, ret_ref), (w_any, w_ref)], sems)
    agg = dense_product(cols_ref, tiles_ref, pieces, refs[-PIECES:], piece_sems, copies[:2])
    for c in copies[2:]:
        c.wait()
    for g in range(8):
        agg += dot(sel_ref[:, g * TILE : (g + 1) * TILE], ret_ref[g, :TILE])
    out_ref[...] = dot(agg.astype(BF), w_ref[...], 1, 1).astype(BF)


HBM = pl.BlockSpec(memory_space=pltpu.HBM)
VMEM = pl.BlockSpec(memory_space=pltpu.VMEM)
DMA = pltpu.SemaphoreType.DMA


def call(kernel, ins, outs, scratch, name, flops, pieces=()):
    many = isinstance(outs, list)
    moved = sum(v.size * v.dtype.itemsize for v in list(ins) + (outs if many else [outs]))
    return pl.pallas_call(
        kernel,
        out_shape=outs,
        in_specs=[HBM] * (len(ins) + len(pieces)),
        out_specs=[VMEM] * len(outs) if many else VMEM,
        scratch_shapes=scratch + [pltpu.VMEM(p.shape, BF) for p in pieces],
        compiler_params=pltpu.CompilerParams(vmem_limit_bytes=VMEM_LIMIT),
        cost_estimate=pl.CostEstimate(flops=flops, bytes_accessed=moved, transcendentals=0),
        name=name,
    )(*ins, *pieces)


def body(
    features,
    weight,
    cotangent,
    dense_tiles,
    dense_cols,
    sparse_tiles,
    sparse_rows,
    sparse_cols,
    send_rows,
    send_counts,
):
    shape = jax.ShapeDtypeStruct
    own = features[0]
    ints, tiles = dense_cols[0, 0], dense_tiles[0, 0]
    square = (256, 256)
    sel, outgoing = call(
        select_kernel,
        [send_counts[0, 0], send_rows[0, 0], own],
        [shape((256, 1024), BF), shape((8, TILE, 256), BF)],
        [pltpu.SMEM((8,), jnp.int32), pltpu.VMEM((8, TILE), jnp.int32), pltpu.VMEM(square, BF), DMA((3,))],
        "select",
        2 * 1024 * 256 * 256,
    )
    received = lax.all_to_all(outgoing, "grp", 0, 0, tiled=True).reshape(1024, 256)
    held = []

    def forward_hook(i, values):
        if i == SELECT_AT:

            held.extend([sel, received])
        if i == 4:
            rec = tie(held[1], values)
            held.extend(
                call(
                    sparse_kernel,
                    [sparse_rows[0, 0], sparse_cols[0, 0], sparse_tiles[0, 0], rec],
                    [shape((256, 2048), BF), shape(square, F32)],
                    [
                        pltpu.SMEM((32,), jnp.int32),
                        pltpu.SMEM((32,), jnp.int32),
                        pltpu.VMEM((32, TILE, TILE), BF),
                        pltpu.VMEM((1024, 256), BF),
                        pltpu.VMEM((16, TILE, TILE), F32),
                        DMA((4,)),
                    ],
                    "sparse",
                    2 * 256 * 2048 * 256,
                )
            )
        return values

    pieces = gather(own, forward_hook)
    sel, _, sparse, sparse_sum = held
    dense_scratch = [pltpu.SMEM((64,), jnp.int32), pltpu.VMEM((64, TILE, TILE), BF)]
    hidden, grad, back = call(
        forward_kernel,
        [ints, tiles, sparse, sparse_sum, weight, cotangent[0]],
        [shape(square, BF), shape(square, BF), shape((8, TILE + 64, 256), BF)],
        dense_scratch
        + [pltpu.VMEM((256, 2048), BF), pltpu.VMEM(square, F32), pltpu.VMEM(square, BF), pltpu.VMEM(square, BF), DMA((6,)), DMA((PIECES,))],
        "forward",
        2 * 256 * 4096 * 256,
        pieces,
    )
    returned = lax.all_to_all(back, "grp", 0, 0, tiled=True)
    part = []

    def add_partner(step, done):
        value = tie(part[0], done)
        part[0] = value + lax.ppermute(value, "blk", [(i, i ^ (1 << step)) for i in range(NX * NZ)])

    def backward_hook(i, values):
        if i == 3:
            part.append(jnp.sum(returned[:, TILE:].astype(F32).reshape(8, 2, 32, 256), axis=(0, 1)))
            add_partner(0, values)
        if i == 4:
            add_partner(1, values)
            add_partner(2, part[0])
        if i == 5:
            add_partner(3, values)
        if i == 6:
            add_partner(4, values)
        return values

    grad_pieces = gather(grad, backward_hook)
    total = part[0] * float(65536) ** -0.5
    grad_weight = lax.all_to_all(jnp.broadcast_to(total[None], (8, 32, 256)), "grp", 0, 0, tiled=True)
    grad_features = call(
        backward_kernel,
        [ints, tiles, sel, returned, weight],
        shape(square, BF),
        dense_scratch + [pltpu.VMEM((256, 1024), BF), pltpu.VMEM((8, TILE + 64, 256), BF), pltpu.VMEM(square, BF), DMA((5,)), DMA((PIECES,))],
        "backward",
        2 * 256 * 4096 * 256,
        grad_pieces,
    )
    return hidden[None], grad_features[None], grad_weight.reshape(256, 256)


def solution(mesh):
    three, four = P("grp", "blk", None), P("grp", "blk", None, None)
    five = P("grp", "blk", None, None, None)
    return jax.shard_map(
        body,
        mesh=mesh,
        in_specs=(three, P(), three, five, three, five, three, three, four, three),
        out_specs=(three, three, P()),
        check_vma=False,
    )
```

time: 183 us -> 140 us (0.77)
  local copies, waits for them, and re-layouts: 35 us -> 3.99 us
  starting transfers between devices: 92.8 us -> 71.1 us
  waiting for transfers between devices: 39 us -> 44.7 us
  Pallas kernels: 12.5 us -> 16.5 us
    unnamed x104 -> x47, local copies, waits for them, and re-layouts: 28.9 us -> 3.22 us
    ppermute x32 -> x12, starting transfers between devices: 32.7 us -> 20.9 us  [go_z(): return lax.ppermute(v, 'blk', swap_z(kind))]
    ppermute x32 -> x12, waiting for transfers between devices: 19.3 us -> 12 us  [go_z(): return lax.ppermute(v, 'blk', swap_z(kind))]
    all_to_all x3 -> x2, starting transfers between devices: 22.1 us -> 15 us  [the longest x1 8.95 us: body(): lax.all_to_all(jnp.broadcast_to(total[None], (8, 32, 256)), 'grp', 0, 0,...]
    all_to_all x1, waiting for transfers between devices: 0.01 us -> 6.72 us  [body(): lax.all_to_all(outgoing, 'grp', 0, 0, tiled=True).reshape(1024, 256)]
    ppermute x16 -> x18, waiting for transfers between devices: 5.27 us -> 11.8 us  [go_x(): return lax.ppermute(v, 'blk', swap_x(kind))]
    all_to_all x1, starting transfers between devices: 12.2 us -> 6.88 us  [body(): lax.all_to_all(outgoing, 'grp', 0, 0, tiled=True).reshape(1024, 256)]
    slice x18 -> x0, local copies, waits for them, and re-layouts: 5.32 us -> none  [the longest x8 2.96 us: ring_x(): return [v, up, down, go_x(down[:h], 0), go_x(up[h:], 1)]]
  transfers between devices with their start and end apart: 57 -> 40, of which waited for: 18 -> 18; matrix products, arithmetic and copies ran while one was open for 4% -> 3% of each run, Pallas kernels for 3% -> 8%
where the time goes in v2:
time: 140 us; the launch traced here: 139 us
  starting transfers between devices  71.1 us (51%)
  waiting for transfers between devices  44.7 us (32%)
  Pallas kernels  16.5 us (12%)
  local copies, waits for them, and re-layouts  3.99 us (3%)
  other arithmetic  1.8 us (1%)
    ppermute x12, starting transfers between devices, go_z(): return lax.ppermute(v, 'blk', swap_z(kind))  20.9 us
    ppermute x18, starting transfers between devices, go_x(): return lax.ppermute(v, 'blk', swap_x(kind))  20.2 us
    pallas_call x4, Pallas kernels, call(): pl.pallas_call(kernel, out_shape=outs, in_specs=[HBM] * (len(ins) + len(p...  16.5 us
    ppermute x5, waiting for transfers between devices, add_partner(): lax.ppermute(value, 'blk', [(i, i ^ 1 << step) for i in range(NX * NZ)])  12.2 us
    ppermute x12, waiting for transfers between devices, go_z(): return lax.ppermute(v, 'blk', swap_z(kind))  12 us
    ppermute x18, waiting for transfers between devices, go_x(): return lax.ppermute(v, 'blk', swap_x(kind))  11.8 us
    all_to_all x1, starting transfers between devices, body(): lax.all_to_all(jnp.broadcast_to(total[None], (8, 32, 256)), 'grp', 0, 0,...  8.95 us
    all_to_all x1, starting transfers between devices, body(): lax.all_to_all(outgoing, 'grp', 0, 0, tiled=True).reshape(1024, 256)  6.88 us
  transfers between devices with their start and end apart: 40, of which 18 were waited for; matrix products, arithmetic and copies ran while one was open for 3% of the time, Pallas kernels for 8%

profile of v2, /device:TPU:1, one launch (start us, length us, event | category | flops | bytes accessed | tf_op | source)
XLA Modules:
  0.0 139.2 jit_solution(11752659105604600603)
XLA Ops:
  0.6 2.6 %collective-permute-start.2 = (bf16[256,256]{1,0:T(8,128)(2,1)}, bf16[256,256]{1,0:T(8,128)(2,1)S(1)}, u32[]{:S(2)}, u32[]{:S(2)}) collective-permute-start(bf16[256,256]{1,0:T(8,128)(2,1)} %bitcast.22), channel_id=1, source_target_pairs={{0,8},{8,0},{16,24},{24,16},{32,40},{40,32},{48,56},{56,48},{64,72... | collective-permute-start | bytes 393224 | tf_op jit(solution)/shard_map/ppermute | solution.py:36
  3.2 4.7 %collective-permute-start = (bf16[256,256]{1,0:T(8,128)(2,1)}, bf16[256,256]{1,0:T(8,128)(2,1)S(1)}, u32[]{:S(2)}, u32[]{:S(2)}) collective-permute-start(bf16[256,256]{1,0:T(8,128)(2,1)} %bitcast.23), channel_id=1, source_target_pairs={{0,56},{8,16},{16,8},{24,32},{32,24},{40,48},{48,40},{56,0},{64,12... | collective-permute-start | bytes 393224 | tf_op jit(solution)/shard_map/ppermute | solution.py:36
  7.9 3.8 %collective-permute-start.3 = (bf16[256,256]{1,0:T(8,128)(2,1)S(1)}, bf16[256,256]{1,0:T(8,128)(2,1)S(1)}, u32[]{:S(2)}, u32[]{:S(2)}) collective-permute-start(bf16[256,256]{1,0:T(8,128)(2,1)S(1)} %collective-permute-done.2), channel_id=1, source_target_pairs={{0,56},{8,16},{16,8},{24,32},{32,24},{40,48},{48,40},{56,0},{64,12... | collective-permute-start | bytes 393224 | tf_op jit(solution)/shard_map/ppermute | solution.py:36
  11.7 2.8 %collective-permute-start.4 = (bf16[256,256]{1,0:T(8,128)(2,1)}, bf16[256,256]{1,0:T(8,128)(2,1)S(1)}, u32[]{:S(2)}, u32[]{:S(2)}) collective-permute-start(bf16[256,256]{1,0:T(8,128)(2,1)} %bitcast.24), channel_id=1, source_target_pairs={{0,32},{8,40},{16,48},{24,56},{32,0},{40,8},{48,16},{56,24},{64,96... | collective-permute-start | bytes 393224 | tf_op jit(solution)/shard_map/ppermute | solution.py:44
  15.5 2.6 %collective-permute-start.8 = (bf16[768,256]{1,0:T(8,128)(2,1)S(1)}, bf16[768,256]{1,0:T(8,128)(2,1)S(1)}, u32[]{:S(2)}, u32[]{:S(2)}) collective-permute-start(bf16[768,256]{1,0:T(8,128)(2,1)S(1)} %pad_maximum_fusion.refs_6_), channel_id=1, source_target_pairs={{0,192},{8,200},{16,208},{24,216},{32,224},{40,232},{48,240},{56,2... | collective-permute-start | bytes 1179656 | tf_op jit(solution)/shard_map/ppermute | solution.py:40
  20.6 2.6 %collective-permute-start.6 = (bf16[768,256]{1,0:T(8,128)(2,1)S(1)}, bf16[768,256]{1,0:T(8,128)(2,1)S(1)}, u32[]{:S(2)}, u32[]{:S(2)}) collective-permute-start(bf16[768,256]{1,0:T(8,128)(2,1)S(1)} %constant_dynamic-update-slice_fusion.refs_10_), channel_id=1, source_target_pairs={{0,192},{8,200},{16,208},{24,216},{32,224},{40,232},{48,240},{56,2... | collective-permute-start | bytes 1179656 | tf_op jit(solution)/shard_map/ppermute | solution.py:40
  23.2 2.6 %collective-permute-done.11 = bf16[256,256]{1,0:T(8,128)(2,1)S(1)} collective-permute-done((bf16[256,256]{1,0:T(8,128)(2,1)S(1)}, bf16[256,256]{1,0:T(8,128)(2,1)S(1)}, u32[]{:S(2)}, u32[]{:S(2)}) %collective-permute-start.11) | collective-permute-done | bytes 131104 | tf_op jit(solution)/shard_map/ppermute | solution.py:36
  27.1 4.0 %collective-permute-done.12 = bf16[256,256]{1,0:T(8,128)(2,1)S(1)} collective-permute-done((bf16[256,256]{1,0:T(8,128)(2,1)S(1)}, bf16[256,256]{1,0:T(8,128)(2,1)S(1)}, u32[]{:S(2)}, u32[]{:S(2)}) %collective-permute-start.12) | collective-permute-done | bytes 131104 | tf_op jit(solution)/shard_map/ppermute | solution.py:36
  31.1 2.6 %collective-permute-start.14 = (bf16[512,256]{1,0:T(8,128)(2,1)S(1)}, bf16[512,256]{1,0:T(8,128)(2,1)}, u32[]{:S(2)}, u32[]{:S(2)}) collective-permute-start(bf16[512,256]{1,0:T(8,128)(2,1)S(1)} %constant_dynamic-update-slice_fusion.3.refs_14_), channel_id=1, source_target_pairs={{0,192},{8,200},{16,208},{24,216},{32,224},{40,232},{48,240},{56,2... | collective-permute-start | bytes 786440 | tf_op jit(solution)/shard_map/ppermute | solution.py:40
  33.7 2.3 %select.1 = (bf16[256,1024]{1,0:T(8,128)(2,1)}, bf16[8,128,256]{2,1,0:T(8,128)(2,1)}) custom-call(s32[8]{0:T(128)} %bitcast.33, s32[8,128]{1,0:T(8,128)} %bitcast.32, bf16[256,256]{1,0:T(8,128)(2,1)} %bitcast.26), custom_call_target="tpu_custom_call" | custom-call | flops 134217728 | bytes 1183776 | tf_op jit(solution)/shard_map/select/pallas_call | solution.py:285
  35.9 6.9 %all-to-all-start = ((bf16[8,128,256]{2,1,0:T(8,128)(2,1)}), bf16[8,128,256]{2,1,0:T(8,128)(2,1)S(1)}, u32[]{:S(2)}, u32[]{:S(2)}) async-start(bf16[8,128,256]{2,1,0:T(8,128)(2,1)} %get-tuple-element.21), calls=%async_computation | async-start | bytes 1048576 | tf_op jit(solution)/shard_map/all_to_all | solution.py:321
  45.6 6.7 %all-to-all-done = bf16[8,128,256]{2,1,0:T(8,128)(2,1)S(1)} async-done(((bf16[8,128,256]{2,1,0:T(8,128)(2,1)}), bf16[8,128,256]{2,1,0:T(8,128)(2,1)S(1)}, u32[]{:S(2)}, u32[]{:S(2)}) %all-to-all-start) | async-done | bytes 524320 | tf_op jit(solution)/shard_map/all_to_all | solution.py:321
  53.1 3.0 %sparse.1 = (bf16[256,2048]{1,0:T(8,128)(2,1)}, f32[256,256]{1,0:T(8,128)}) custom-call(s32[32]{0:T(128)} %bitcast.29, s32[32]{0:T(128)} %bitcast.30, bf16[32,128,128]{2,1,0:T(8,128)(2,1)} %bitcast.17, bf16[1024,256]{1,0:T(8,128)(2,1)} %bitcast.16), custom_call_target="tpu_custom_call" | custom-call | flops 268435456 | bytes 2883840 | tf_op jit(solution)/shard_map/sparse/pallas_call | solution.py:285
  56.1 3.4 %collective-permute-done.15.refs_17_ = bf16[512,256]{1,0:T(8,128)(2,1)} collective-permute-done((bf16[512,256]{1,0:T(8,128)(2,1)}, bf16[512,256]{1,0:T(8,128)(2,1)}, u32[]{:S(2)}, u32[]{:S(2)}) %collective-permute-start.15) | collective-permute-done | bytes 262176 | tf_op jit(solution)/shard_map/ppermute | solution.py:40
  60.2 5.8 %forward.1 = (bf16[256,256]{1,0:T(8,128)(2,1)}, bf16[256,256]{1,0:T(8,128)(2,1)}, bf16[8,192,256]{2,1,0:T(8,128)(2,1)}) custom-call(s32[64]{0:T(128)} %bitcast.27, bf16[64,128,128]{2,1,0:T(8,128)(2,1)} %bitcast.14, bf16[256,2048]{1,0:T(8,128)(2,1)} %get-tuple-element.23.refs_2_, f32[256,256]{1,0:T(8,128)} %get-tuple-element.24.refs_3_, ...), custom_call_target="tpu_custom_call" | custom-call | flops 536870912 | bytes 4718848 | tf_op jit(solution)/shard_map/forward/pallas_call | solution.py:285
  71.0 6.1 %all-to-all-start.1 = ((bf16[8,192,256]{2,1,0:T(8,128)(2,1)}), bf16[8,192,256]{2,1,0:T(8,128)(2,1)S(1)}, u32[]{:S(2)}, u32[]{:S(2)}) async-start(bf16[8,192,256]{2,1,0:T(8,128)(2,1)} %get-tuple-element.30), calls=%async_computation.1 | async-start | bytes 1572864 | tf_op jit(solution)/shard_map/all_to_all | solution.py:362
  82.6 2.2 %collective-permute-done.22 = bf16[256,256]{1,0:T(8,128)(2,1)S(1)} collective-permute-done((bf16[256,256]{1,0:T(8,128)(2,1)S(1)}, bf16[256,256]{1,0:T(8,128)(2,1)S(1)}, u32[]{:S(2)}, u32[]{:S(2)}) %collective-permute-start.22) | collective-permute-done | bytes 131104 | tf_op jit(solution)/shard_map/ppermute | solution.py:36
  101.4 3.7 %collective-permute-done.33 = f32[32,256]{1,0:T(8,128)S(1)} collective-permute-done((f32[32,256]{1,0:T(8,128)S(1)}, f32[32,256]{1,0:T(8,128)S(1)}, u32[]{:S(2)}, u32[]{:S(2)}) %collective-permute-start.33) | collective-permute-done | bytes 32800 | tf_op jit(solution)/shard_map/ppermute | solution.py:367
  107.0 4.8 %collective-permute-done.34 = f32[32,256]{1,0:T(8,128)S(1)} collective-permute-done((f32[32,256]{1,0:T(8,128)S(1)}, f32[32,256]{1,0:T(8,128)S(1)}, u32[]{:S(2)}, u32[]{:S(2)}) %collective-permute-start.34) | collective-permute-done | bytes 32800 | tf_op jit(solution)/shard_map/ppermute | solution.py:367
  111.9 3.3 %collective-permute-done.29.refs_14_ = bf16[512,256]{1,0:T(8,128)(2,1)S(1)} collective-permute-done((bf16[512,256]{1,0:T(8,128)(2,1)S(1)}, bf16[512,256]{1,0:T(8,128)(2,1)S(1)}, u32[]{:S(2)}, u32[]{:S(2)}) %collective-permute-start.29) | collective-permute-done | bytes 262176 | tf_op jit(solution)/shard_map/ppermute | solution.py:40
  115.2 2.7 %collective-permute-done.35 = f32[32,256]{1,0:T(8,128)S(1)} collective-permute-done((f32[32,256]{1,0:T(8,128)S(1)}, f32[32,256]{1,0:T(8,128)S(1)}, u32[]{:S(2)}, u32[]{:S(2)}) %collective-permute-start.35) | collective-permute-done | bytes 32800 | tf_op jit(solution)/shard_map/ppermute | solution.py:367
  119.0 2.3 %collective-permute-start.26 = (bf16[768,256]{1,0:T(8,128)(2,1)}, bf16[768,256]{1,0:T(8,128)(2,1)}, u32[]{:S(2)}, u32[]{:S(2)}) collective-permute-start(bf16[768,256]{1,0:T(8,128)(2,1)} %collective-permute-done.24.refs_10_), channel_id=1, source_target_pairs={{0,192},{8,200},{16,208},{24,216},{32,224},{40,232},{48,240},{56,2... | collective-permute-start | bytes 1179656 | tf_op jit(solution)/shard_map/ppermute | solution.py:40
  123.0 9.0 %all-to-all-start.2 = ((f32[8,32,256]{2,1,0:T(8,128)}), f32[8,32,256]{2,1,0:T(8,128)S(1)}, u32[]{:S(2)}, u32[]{:S(2)}) async-start(f32[8,32,256]{2,1,0:T(8,128)} %broadcast_in_dim.14), calls=%async_computation.2 | async-start | bytes 524288 | tf_op jit(solution)/shard_map/all_to_all | solution.py:384
  132.0 5.5 %backward.1 = bf16[256,256]{1,0:T(8,128)(2,1)} custom-call(s32[64]{0:T(128)} %bitcast.28, bf16[64,128,128]{2,1,0:T(8,128)(2,1)} %bitcast.15, bf16[256,1024]{1,0:T(8,128)(2,1)} %get-tuple-element.29.refs_2_, bf16[8,192,256]{2,1,0:T(8,128)(2,1)} %copy-done, bf16[256,256]{1,0:T(8,128)(2,1)} %refs_4_.3, bf16[768,256]{1,0:T(8,128)(2,1)} %copy-done.3, ...), custom_call_target="tpu_custom_call" | custom-call | flops 536870912 | bytes 3670272 | tf_op jit(solution)/shard_map/backward/pallas_call | solution.py:285
  (121 shorter events, 42.5 us)
Async XLA Ops:
  7.9 10.2 %collective-permute-start.3 = (bf16[256,256]{1,0:T(8,128)(2,1)S(1)}, bf16[256,256]{1,0:T(8,128)(2,1)S(1)}, u32[]{:S(2)}, u32[]{:S(2)}) collective-permute-start(bf16[256,256]{1,0:T(8,128)(2,1)S(1)} %collective-permute-done.2), channel_id=1, source_target_pairs={{0,56},{8,16},{16,8},{24,32},{32,24},{40,48},{48,40},{56,0},{64,12... | collective-permute-start | bytes 393224 | tf_op jit(solution)/shard_map/ppermute | solution.py:36
  15.5 18.2 %collective-permute-start.8 = (bf16[768,256]{1,0:T(8,128)(2,1)S(1)}, bf16[768,256]{1,0:T(8,128)(2,1)S(1)}, u32[]{:S(2)}, u32[]{:S(2)}) collective-permute-start(bf16[768,256]{1,0:T(8,128)(2,1)S(1)} %pad_maximum_fusion.refs_6_), channel_id=1, source_target_pairs={{0,192},{8,200},{16,208},{24,216},{32,224},{40,232},{48,240},{56,2... | collective-permute-start | bytes 1179656 | tf_op jit(solution)/shard_map/ppermute | solution.py:40
  18.1 24.8 %collective-permute-start.7 = (bf16[768,256]{1,0:T(8,128)(2,1)S(1)}, bf16[768,256]{1,0:T(8,128)(2,1)S(1)}, u32[]{:S(2)}, u32[]{:S(2)}) collective-permute-start(bf16[768,256]{1,0:T(8,128)(2,1)S(1)} %pad_maximum_fusion.refs_6_), channel_id=1, source_target_pairs={{0,64},{8,72},{16,80},{24,88},{32,96},{40,104},{48,112},{56,120},{... | collective-permute-start | bytes 1179656 | tf_op jit(solution)/shard_map/ppermute | solution.py:40
  20.6 23.8 %collective-permute-start.6 = (bf16[768,256]{1,0:T(8,128)(2,1)S(1)}, bf16[768,256]{1,0:T(8,128)(2,1)S(1)}, u32[]{:S(2)}, u32[]{:S(2)}) collective-permute-start(bf16[768,256]{1,0:T(8,128)(2,1)S(1)} %constant_dynamic-update-slice_fusion.refs_10_), channel_id=1, source_target_pairs={{0,192},{8,200},{16,208},{24,216},{32,224},{40,232},{48,240},{56,2... | collective-permute-start | bytes 1179656 | tf_op jit(solution)/shard_map/ppermute | solution.py:40
  23.2 21.3 %collective-permute-start.5 = (bf16[768,256]{1,0:T(8,128)(2,1)S(1)}, bf16[768,256]{1,0:T(8,128)(2,1)S(1)}, u32[]{:S(2)}, u32[]{:S(2)}) collective-permute-start(bf16[768,256]{1,0:T(8,128)(2,1)S(1)} %constant_dynamic-update-slice_fusion.refs_10_), channel_id=1, source_target_pairs={{0,64},{8,72},{16,80},{24,88},{32,96},{40,104},{48,112},{56,120},{... | collective-permute-start | bytes 1179656 | tf_op jit(solution)/shard_map/ppermute | solution.py:40
  31.1 13.9 %collective-permute-start.14 = (bf16[512,256]{1,0:T(8,128)(2,1)S(1)}, bf16[512,256]{1,0:T(8,128)(2,1)}, u32[]{:S(2)}, u32[]{:S(2)}) collective-permute-start(bf16[512,256]{1,0:T(8,128)(2,1)S(1)} %constant_dynamic-update-slice_fusion.3.refs_14_), channel_id=1, source_target_pairs={{0,192},{8,200},{16,208},{24,216},{32,224},{40,232},{48,240},{56,2... | collective-permute-start | bytes 786440 | tf_op jit(solution)/shard_map/ppermute | solution.py:40
  33.6 11.4 %collective-permute-start.13 = (bf16[512,256]{1,0:T(8,128)(2,1)S(1)}, bf16[512,256]{1,0:T(8,128)(2,1)}, u32[]{:S(2)}, u32[]{:S(2)}) collective-permute-start(bf16[512,256]{1,0:T(8,128)(2,1)S(1)} %constant_dynamic-update-slice_fusion.3.refs_14_), channel_id=1, source_target_pairs={{0,64},{8,72},{16,80},{24,88},{32,96},{40,104},{48,112},{56,120},{... | collective-permute-start | bytes 786440 | tf_op jit(solution)/shard_map/ppermute | solution.py:40
  35.9 16.4 %all-to-all-start = ((bf16[8,128,256]{2,1,0:T(8,128)(2,1)}), bf16[8,128,256]{2,1,0:T(8,128)(2,1)S(1)}, u32[]{:S(2)}, u32[]{:S(2)}) async-start(bf16[8,128,256]{2,1,0:T(8,128)(2,1)} %get-tuple-element.21), calls=%async_computation | async-start | bytes 1048576 | tf_op jit(solution)/shard_map/all_to_all | solution.py:321
  42.8 16.7 %collective-permute-start.9 = (bf16[768,256]{1,0:T(8,128)(2,1)S(1)}, bf16[768,256]{1,0:T(8,128)(2,1)S(1)}, u32[]{:S(2)}, u32[]{:S(2)}) collective-permute-start(bf16[768,256]{1,0:T(8,128)(2,1)S(1)} %collective-permute-done.8.refs_8_), channel_id=1, source_target_pairs={{0,64},{8,72},{16,80},{24,88},{32,96},{40,104},{48,112},{56,120},{... | collective-permute-start | bytes 1179656 | tf_op jit(solution)/shard_map/ppermute | solution.py:40
  44.4 15.1 %collective-permute-start.10 = (bf16[768,256]{1,0:T(8,128)(2,1)S(1)}, bf16[768,256]{1,0:T(8,128)(2,1)}, u32[]{:S(2)}, u32[]{:S(2)}) collective-permute-start(bf16[768,256]{1,0:T(8,128)(2,1)S(1)} %collective-permute-done.5.refs_11_), channel_id=1, source_target_pairs={{0,192},{8,200},{16,208},{24,216},{32,224},{40,232},{48,240},{56,2... | collective-permute-start | bytes 1179656 | tf_op jit(solution)/shard_map/ppermute | solution.py:40
  45.0 14.5 %collective-permute-start.15 = (bf16[512,256]{1,0:T(8,128)(2,1)}, bf16[512,256]{1,0:T(8,128)(2,1)}, u32[]{:S(2)}, u32[]{:S(2)}) collective-permute-start(bf16[512,256]{1,0:T(8,128)(2,1)} %collective-permute-done.14.refs_16_), channel_id=1, source_target_pairs={{0,64},{8,72},{16,80},{24,88},{32,96},{40,104},{48,112},{56,120},{... | collective-permute-start | bytes 786440 | tf_op jit(solution)/shard_map/ppermute | solution.py:40
  66.0 12.0 %collective-permute-start.17 = (bf16[256,256]{1,0:T(8,128)(2,1)}, bf16[256,256]{1,0:T(8,128)(2,1)S(1)}, u32[]{:S(2)}, u32[]{:S(2)}) collective-permute-start(bf16[256,256]{1,0:T(8,128)(2,1)} %get-tuple-element.31), channel_id=1, source_target_pairs={{0,56},{8,16},{16,8},{24,32},{32,24},{40,48},{48,40},{56,0},{64,12... | collective-permute-start | bytes 393224 | tf_op jit(solution)/shard_map/ppermute | solution.py:36
  67.9 10.8 %collective-permute-start.16 = (bf16[256,256]{1,0:T(8,128)(2,1)}, bf16[256,256]{1,0:T(8,128)(2,1)S(1)}, u32[]{:S(2)}, u32[]{:S(2)}) collective-permute-start(bf16[256,256]{1,0:T(8,128)(2,1)} %get-tuple-element.31), channel_id=1, source_target_pairs={{0,8},{8,0},{16,24},{24,16},{32,40},{40,32},{48,56},{56,48},{64,72... | collective-permute-start | bytes 393224 | tf_op jit(solution)/shard_map/ppermute | solution.py:36
  69.0 15.8 %collective-permute-start.23 = (bf16[256,256]{1,0:T(8,128)(2,1)}, bf16[256,256]{1,0:T(8,128)(2,1)S(1)}, u32[]{:S(2)}, u32[]{:S(2)}) collective-permute-start(bf16[256,256]{1,0:T(8,128)(2,1)} %get-tuple-element.31), channel_id=1, source_target_pairs={{0,32},{8,40},{16,48},{24,56},{32,0},{40,8},{48,16},{56,24},{64,96... | collective-permute-start | bytes 393224 | tf_op jit(solution)/shard_map/ppermute | solution.py:44
  71.0 21.8 %all-to-all-start.1 = ((bf16[8,192,256]{2,1,0:T(8,128)(2,1)}), bf16[8,192,256]{2,1,0:T(8,128)(2,1)S(1)}, u32[]{:S(2)}, u32[]{:S(2)}) async-start(bf16[8,192,256]{2,1,0:T(8,128)(2,1)} %get-tuple-element.30), calls=%async_computation.1 | async-start | bytes 1572864 | tf_op jit(solution)/shard_map/all_to_all | solution.py:362
  80.5 11.4 %collective-permute-start.19 = (bf16[768,256]{1,0:T(8,128)(2,1)S(1)}, bf16[768,256]{1,0:T(8,128)(2,1)S(1)}, u32[]{:S(2)}, u32[]{:S(2)}) collective-permute-start(bf16[768,256]{1,0:T(8,128)(2,1)S(1)} %constant_dynamic-update-slice_fusion.5.refs_5_), channel_id=1, source_target_pairs={{0,192},{8,200},{16,208},{24,216},{32,224},{40,232},{48,240},{56,2... | collective-permute-start | bytes 1179656 | tf_op jit(solution)/shard_map/ppermute | solution.py:40
  84.9 15.5 %collective-permute-start.25 = (bf16[768,256]{1,0:T(8,128)(2,1)S(1)}, bf16[768,256]{1,0:T(8,128)(2,1)S(1)}, u32[]{:S(2)}, u32[]{:S(2)}) collective-permute-start(bf16[768,256]{1,0:T(8,128)(2,1)S(1)} %constant_dynamic-update-slice_fusion.8.refs_9_), channel_id=1, source_target_pairs={{0,192},{8,200},{16,208},{24,216},{32,224},{40,232},{48,240},{56,2... | collective-permute-start | bytes 1179656 | tf_op jit(solution)/shard_map/ppermute | solution.py:40
  86.8 14.4 %collective-permute-start.24 = (bf16[768,256]{1,0:T(8,128)(2,1)S(1)}, bf16[768,256]{1,0:T(8,128)(2,1)}, u32[]{:S(2)}, u32[]{:S(2)}) collective-permute-start(bf16[768,256]{1,0:T(8,128)(2,1)S(1)} %constant_dynamic-update-slice_fusion.8.refs_9_), channel_id=1, source_target_pairs={{0,64},{8,72},{16,80},{24,88},{32,96},{40,104},{48,112},{56,120},{... | collective-permute-start | bytes 1179656 | tf_op jit(solution)/shard_map/ppermute | solution.py:40
  92.7 25.2 %collective-permute-start.20 = (bf16[768,256]{1,0:T(8,128)(2,1)S(1)}, bf16[768,256]{1,0:T(8,128)(2,1)}, u32[]{:S(2)}, u32[]{:S(2)}) collective-permute-start(bf16[768,256]{1,0:T(8,128)(2,1)S(1)} %collective-permute-done.19.refs_7_), channel_id=1, source_target_pairs={{0,64},{8,72},{16,80},{24,88},{32,96},{40,104},{48,112},{56,120},{... | collective-permute-start | bytes 1179656 | tf_op jit(solution)/shard_map/ppermute | solution.py:40
  94.2 17.6 %collective-permute-start.30 = (bf16[512,256]{1,0:T(8,128)(2,1)S(1)}, bf16[512,256]{1,0:T(8,128)(2,1)S(1)}, u32[]{:S(2)}, u32[]{:S(2)}) collective-permute-start(bf16[512,256]{1,0:T(8,128)(2,1)S(1)} %constant_dynamic-update-slice_fusion.11.refs_13_), channel_id=1, source_target_pairs={{0,192},{8,200},{16,208},{24,216},{32,224},{40,232},{48,240},{56,2... | collective-permute-start | bytes 786440 | tf_op jit(solution)/shard_map/ppermute | solution.py:40
  96.1 19.0 %collective-permute-start.29 = (bf16[512,256]{1,0:T(8,128)(2,1)S(1)}, bf16[512,256]{1,0:T(8,128)(2,1)S(1)}, u32[]{:S(2)}, u32[]{:S(2)}) collective-permute-start(bf16[512,256]{1,0:T(8,128)(2,1)S(1)} %constant_dynamic-update-slice_fusion.11.refs_13_), channel_id=1, source_target_pairs={{0,64},{8,72},{16,80},{24,88},{32,96},{40,104},{48,112},{56,120},{... | collective-permute-start | bytes 786440 | tf_op jit(solution)/shard_map/ppermute | solution.py:40
  119.0 13.0 %collective-permute-start.31 = (bf16[512,256]{1,0:T(8,128)(2,1)S(1)}, bf16[512,256]{1,0:T(8,128)(2,1)}, u32[]{:S(2)}, u32[]{:S(2)}) collective-permute-start(bf16[512,256]{1,0:T(8,128)(2,1)S(1)} %collective-permute-done.30.refs_15_), channel_id=1, source_target_pairs={{0,64},{8,72},{16,80},{24,88},{32,96},{40,104},{48,112},{56,120},{... | collective-permute-start | bytes 786440 | tf_op jit(solution)/shard_map/ppermute | solution.py:40
  119.0 13.0 %collective-permute-start.26 = (bf16[768,256]{1,0:T(8,128)(2,1)}, bf16[768,256]{1,0:T(8,128)(2,1)}, u32[]{:S(2)}, u32[]{:S(2)}) collective-permute-start(bf16[768,256]{1,0:T(8,128)(2,1)} %collective-permute-done.24.refs_10_), channel_id=1, source_target_pairs={{0,192},{8,200},{16,208},{24,216},{32,224},{40,232},{48,240},{56,2... | collective-permute-start | bytes 1179656 | tf_op jit(solution)/shard_map/ppermute | solution.py:40
  123.0 15.5 %all-to-all-start.2 = ((f32[8,32,256]{2,1,0:T(8,128)}), f32[8,32,256]{2,1,0:T(8,128)S(1)}, u32[]{:S(2)}, u32[]{:S(2)}) async-start(f32[8,32,256]{2,1,0:T(8,128)} %broadcast_in_dim.14), calls=%async_computation.2 | async-start | bytes 524288 | tf_op jit(solution)/shard_map/all_to_all | solution.py:384
  (35 other events, 598.9 us)

commit v3 on v2

v3 whole, which is shorter than its diff:
```python
import jax
import jax.numpy as jnp
from jax import lax
from jax.experimental import pallas as pl
from jax.experimental.pallas import tpu as pltpu
from jax.sharding import PartitionSpec as P

NX, NZ = 4, 8
TILE = 128
SELECT_AT = 2
BF = jnp.bfloat16
F32 = jnp.float32
VMEM_LIMIT = 58 * 1024 * 1024


def swap_z(kind):
    def partner(z):
        if kind == 0:
            return z ^ 1
        return (z - 1) % NZ if z % 2 == 0 else (z + 1) % NZ

    return [(x * NZ + z, x * NZ + partner(z)) for x in range(NX) for z in range(NZ)]


def swap_x(kind):
    def partner(x):
        if kind == 0:
            return x ^ 1
        return (x - 1) % NX if x % 2 == 0 else (x + 1) % NX

    return [(x * NZ + z, partner(x) * NZ + z) for x in range(NX) for z in range(NZ)]


def go_z(v, kind):
    return lax.ppermute(v, "blk", swap_z(kind))


def go_x(v, kind):
    return lax.ppermute(v, "blk", swap_x(kind))


def tie(values, *others):
    return lax.optimization_barrier((values, others))[0]


def gather(v, hook):
    u1, d1 = go_z(v, 0), go_z(v, 1)
    u1, d1 = hook(0, (u1, d1))
    u2, d2 = go_z(d1, 0), go_z(u1, 1)
    p = jnp.concatenate([v, u1, d1])
    pu, pd = go_x(p, 0), go_x(p, 1)
    u2, d2 = hook(1, (u2, d2))
    u3, d3 = go_z(d2, 0), go_z(u2, 1)
    q = jnp.concatenate([u2, d2])
    qu, qd = go_x(q, 0), go_x(q, 1)
    u3, d3 = hook(2, (u3, d3))
    t = go_z(d3, 0)
    r = jnp.concatenate([u3, d3])
    ru, rd = go_x(r, 0), go_x(r, 1)
    pu, pd = hook(3, (pu, pd))
    px = go_x(tie(pd, pu), 0)
    qu, qd = hook(4, (qu, qd))
    qx = go_x(tie(qu, qd), 1)
    hook(6, [p, pu, pd, q, qu, qd, t])
    t = hook(7, t)
    tu, td = go_x(t, 0), go_x(t, 1)
    ru, rd = hook(5, (ru, rd))
    rx = go_x(tie(rd, ru), 0)
    tu, td = hook(8, (tu, td))
    tx = go_x(tie(tu, td), 1)
    hook(9, (px, tu, td))
    hook(10, (qx, tx))
    hook(11, rx)
    return [p, pu, pd, px, q, qu, qd, qx, r, ru, rd, rx, t, tu, td, tx]


def dot(a, b, ca=1, cb=0):
    return lax.dot_general(a, b, (((ca,), (cb,)), ((), ())), preferred_element_type=F32)


def load(pairs, sems):
    copies = [pltpu.make_async_copy(src, dst, sems.at[i]) for i, (src, dst) in enumerate(pairs)]
    for c in copies:
        c.start()
    return copies


def select_kernel(count_any, rows_any, x_any, sel_ref, out_ref, count_ref, rows_ref, x_ref, sems):
    for c in load([(count_any, count_ref), (rows_any, rows_ref), (x_any, x_ref)], sems):
        c.wait()
    lane = lax.broadcasted_iota(jnp.int32, (1, TILE), 1)
    row = lax.broadcasted_iota(jnp.int32, (2 * TILE, TILE), 0)
    for s in range(8):
        listed = jnp.where(lane < count_ref[s], rows_ref[s : s + 1, :], -1)
        sel = jnp.where(row == listed, 1.0, 0.0).astype(BF)
        sel_ref[:, s * TILE : (s + 1) * TILE] = sel
        out_ref[s] = dot(sel, x_ref[...], 0, 0).astype(BF)


def sparse_kernel(rows_any, cols_any, tiles_any, rec_any, out_ref, sum_ref, rows_ref, cols_ref, tiles_ref, rec_ref, total, sems):
    copies = load([(rows_any, rows_ref), (cols_any, cols_ref), (tiles_any, tiles_ref), (rec_any, rec_ref)], sems)
    total[...] = jnp.zeros_like(total)
    for c in copies:
        c.wait()
    for u in range(32):
        at = rows_ref[u] * 8 + cols_ref[u]
        total[at] += tiles_ref[u].astype(F32)
    for r in range(2):
        rows = slice(r * TILE, (r + 1) * TILE)
        for q in range(8):
            high, low = split(total[r * 8 + q])
            out_ref[rows, q * TILE : (q + 1) * TILE] = high
            out_ref[rows, (8 + q) * TILE : (9 + q) * TILE] = low
    half = 8 * TILE
    sum_ref[...] = dot(out_ref[:, :half], rec_ref[...]) + dot(out_ref[:, half:], rec_ref[...])


def split(v):
    high = v.astype(BF)
    return high, (v - high.astype(F32)).astype(BF)


EARLY = (0, 1, 2, 4, 5, 6, 12)
ALL = tuple(range(16))
LATE = (3, 7, 8, 9, 10, 11, 13, 14, 15)


def dense_product(ids, cols_ref, cols_copy, tiles_any, tiles_ref, tile_sems, piece_any, pieces, piece_sems):
    blk = lax.axis_index("blk")
    x, z = blk // NZ, blk % NZ
    sx, sz = 1 - 2 * (x % 2), 1 - 2 * (z % 2)
    xs = [lax.rem(x + NX + k * sx, NX) * NZ for k in (0, 1, -1, 2)]
    zs = [[lax.rem(z + NZ + k * sz, NZ) for k in part] for part in ((0, 1, -1), (2, -2), (3, -3), (4,))]
    held = []
    for n, piece in enumerate(ids):
        held += [(xs[piece % 4] + zv, n, 2 * TILE * k) for k, zv in enumerate(zs[piece // 4])]
    tiles = load([(tiles_any.at[pl.ds(2 * c, 2)], tiles_ref.at[pl.ds(2 * n, 2)]) for n, (c, _, _) in enumerate(held)], tile_sems)
    copies = load(list(zip(piece_any, pieces)), piece_sems)
    cols_copy.wait()
    sums = [jnp.zeros((TILE, 2 * TILE), F32) for _ in range(2)]
    waited = set()
    for n in range(0, len(held), 2):
        pair = held[n : n + 2]
        tiles[n].wait()
        tiles[n + 1].wait()
        for _, piece, _ in pair:
            if piece not in waited:
                copies[piece].wait()
                waited.add(piece)
        for r in range(2):
            left = jnp.concatenate([tiles_ref[2 * n + r], tiles_ref[2 * n + 2 + r]], axis=1)
            right = [
                pieces[p][pl.ds(pl.multiple_of(at + cols_ref[2 * c + r] * TILE, TILE), TILE), :] for c, p, at in pair
            ]
            sums[r] = sums[r] + dot(left, jnp.concatenate(right, axis=0))
    return jnp.concatenate(sums, axis=0)


def dense_scratch(pieces):
    blocks = sum(p.shape[0] for p in pieces) // (2 * TILE)
    return [pltpu.SMEM((64,), jnp.int32), pltpu.VMEM((2 * blocks, TILE, TILE), BF), DMA((blocks,)), DMA((len(pieces),))]


def early_kernel(*refs):
    n = len(EARLY)
    cols_any, tiles_any = refs[:2]
    out_ref, sems, cols_ref, tiles_ref, tile_sems, piece_sems = refs[2 + n : 8 + n]
    (cols_copy,) = load([(cols_any, cols_ref)], sems)
    out_ref[...] = dense_product(
        EARLY, cols_ref, cols_copy, tiles_any, tiles_ref, tile_sems, refs[2 : 2 + n], refs[-n:], piece_sems
    )


def forward_kernel(*refs):
    n = len(ALL)
    cols_any, tiles_any, s_any, sum_any, w_any, cot_any = refs[:6]
    hidden_ref, grad_ref, back_ref = refs[6 + n : 9 + n]
    s_ref, sum_ref, w_ref, cot_ref, sems, cols_ref, tiles_ref, tile_sems, piece_sems = refs[9 + n : 18 + n]
    ins = [(cols_any, cols_ref), (sum_any, sum_ref), (w_any, w_ref), (cot_any, cot_ref)]
    copies = load(ins + [(s_any, s_ref)], sems)
    agg = dense_product(
        ALL, cols_ref, copies[0], tiles_any, tiles_ref, tile_sems, refs[6 : 6 + n], refs[-n:], piece_sems
    )
    for c in copies[1:]:
        c.wait()
    half = 8 * TILE
    high, low = split(agg + sum_ref[...])
    pre = dot(high, w_ref[...]) + dot(low, w_ref[...])
    sig = jax.nn.sigmoid(pre)
    hidden_ref[...] = (pre * sig).astype(BF)
    grad = (cot_ref[...].astype(F32) * sig * (1.0 + pre * (1.0 - sig))).astype(BF)
    grad_ref[...] = grad
    slots = (dot(s_ref[:, :half], grad, 0, 0) + dot(s_ref[:, half:], grad, 0, 0)).astype(BF)
    high, low = split((dot(high, grad, 0, 0) + dot(low, grad, 0, 0)) * float(65536) ** -0.5)
    for g in range(8):
        back_ref[g, :TILE] = slots[g * TILE : (g + 1) * TILE]
        back_ref[g, TILE : TILE + 32] = high[g * 32 : (g + 1) * 32]
        back_ref[g, TILE + 32 :] = low[g * 32 : (g + 1) * 32]


def backward_kernel(*refs):
    n = len(LATE)
    cols_any, tiles_any, early_any, sel_any, ret_any, w_any = refs[:6]
    out_ref, early_ref, sel_ref, ret_ref, w_ref, sems, cols_ref, tiles_ref, tile_sems, piece_sems = refs[6 + n : 16 + n]
    ins = [(cols_any, cols_ref), (early_any, early_ref), (sel_any, sel_ref), (ret_any.at[:, pl.ds(0, TILE)], ret_ref)]
    copies = load(ins + [(w_any, w_ref)], sems)
    agg = dense_product(
        LATE, cols_ref, copies[0], tiles_any, tiles_ref, tile_sems, refs[6 : 6 + n], refs[-n:], piece_sems
    )
    for c in copies[1:]:
        c.wait()
    agg += early_ref[...]
    for g in range(8):
        agg += dot(sel_ref[:, g * TILE : (g + 1) * TILE], ret_ref[g])
    out_ref[...] = dot(agg.astype(BF), w_ref[...], 1, 1).astype(BF)


HBM = pl.BlockSpec(memory_space=pltpu.HBM)
VMEM = pl.BlockSpec(memory_space=pltpu.VMEM)
DMA = pltpu.SemaphoreType.DMA


def call(kernel, ins, outs, scratch, name, flops, pieces=()):
    many = isinstance(outs, list)
    moved = sum(v.size * v.dtype.itemsize for v in list(ins) + (outs if many else [outs]))
    return pl.pallas_call(
        kernel,
        out_shape=outs,
        in_specs=[HBM] * (len(ins) + len(pieces)),
        out_specs=[VMEM] * len(outs) if many else VMEM,
        scratch_shapes=scratch + [pltpu.VMEM(p.shape, BF) for p in pieces],
        compiler_params=pltpu.CompilerParams(vmem_limit_bytes=VMEM_LIMIT),
        cost_estimate=pl.CostEstimate(flops=flops, bytes_accessed=moved, transcendentals=0),
        name=name,
    )(*ins, *pieces)


def body(
    features,
    weight,
    cotangent,
    dense_tiles,
    dense_cols,
    sparse_tiles,
    sparse_rows,
    sparse_cols,
    send_rows,
    send_counts,
):
    shape = jax.ShapeDtypeStruct
    own = features[0]
    ints, tiles = dense_cols[0, 0], dense_tiles[0, 0]
    square = (256, 256)
    sel, outgoing = call(
        select_kernel,
        [send_counts[0, 0], send_rows[0, 0], own],
        [shape((256, 1024), BF), shape((8, TILE, 256), BF)],
        [pltpu.SMEM((8,), jnp.int32), pltpu.VMEM((8, TILE), jnp.int32), pltpu.VMEM(square, BF), DMA((3,))],
        "select",
        2 * 1024 * 256 * 256,
    )
    received = lax.all_to_all(outgoing, "grp", 0, 0, tiled=True).reshape(1024, 256)
    held = []

    def early(taken):
        scratch = [DMA((1,))] + dense_scratch(taken)
        return call(early_kernel, [ints, tiles], shape(square, F32), scratch, "early", 2 * 256 * 2048 * 256, taken)

    sums = []

    def forward_hook(i, values):
        if i == SELECT_AT:

            held.extend([sel, received])
        if i == 4:
            rec = tie(held[1], values)
            held.extend(
                call(
                    sparse_kernel,
                    [sparse_rows[0, 0], sparse_cols[0, 0], sparse_tiles[0, 0], rec],
                    [shape((256, 2048), BF), shape(square, F32)],
                    [
                        pltpu.SMEM((32,), jnp.int32),
                        pltpu.SMEM((32,), jnp.int32),
                        pltpu.VMEM((32, TILE, TILE), BF),
                        pltpu.VMEM((1024, 256), BF),
                        pltpu.VMEM((16, TILE, TILE), F32),
                        DMA((4,)),
                    ],
                    "sparse",
                    2 * 256 * 2048 * 256,
                )
            )
        return values

    pieces = gather(own, forward_hook)
    sel, _, sparse, sparse_sum = held

    hidden, grad, back = call(
        forward_kernel,
        [ints, tiles, sparse, sparse_sum, weight, cotangent[0]],
        [shape(square, BF), shape(square, BF), shape((8, TILE + 64, 256), BF)],
        [pltpu.VMEM((256, 2048), BF), pltpu.VMEM(square, F32), pltpu.VMEM(square, BF)]
        + [pltpu.VMEM(square, BF), DMA((5,))]
        + dense_scratch(pieces),
        "forward",
        2 * 256 * 4096 * 256,
        pieces,
    )
    returned = lax.all_to_all(back, "grp", 0, 0, tiled=True)
    part = []

    def add_group(groups, *done):
        value = tie(part[-1], *done)
        n = len(groups[0])
        shared = lax.all_to_all(
            jnp.broadcast_to(value[None], (n, 32, 256)), "blk", 0, 0, axis_index_groups=groups, tiled=True
        )
        part.append(jnp.sum(shared, axis=0))

    def backward_hook(i, values):
        if i == 0:
            part.append(jnp.sum(returned[:, TILE:].astype(F32).reshape(8, 2, 32, 256), axis=(0, 1)))
        if i == 3:
            add_group([[x * NZ + z for x in range(NX)] for z in range(NZ)], values)
        if i == 6:
            sums.append(early(values))
        if i == 8:
            add_group([[x * NZ + z for z in range(NZ)] for x in range(NX)], values)
        if i == 9:
            part.append(tie(part[-1], values, sums[0]))
        if i in (10, 11):
            part.append(tie(part[-1], values))
        return values

    grad_pieces = gather(grad, backward_hook)
    shared = jnp.broadcast_to(part[-1][None], (8, 32, 256))
    grad_weight = lax.all_to_all(shared, "grp", 0, 0, tiled=True)
    taken = [grad_pieces[i] for i in LATE]
    grad_features = call(
        backward_kernel,
        [ints, tiles, sums[0], sel, returned, weight],
        shape(square, BF),
        [pltpu.VMEM(square, F32), pltpu.VMEM((256, 1024), BF), pltpu.VMEM((8, TILE, 256), BF), pltpu.VMEM(square, BF)]
        + [DMA((5,))]
        + dense_scratch(taken),
        "backward",
        2 * 256 * 2048 * 256,
        taken,
    )
    return hidden[None], grad_features[None], grad_weight.reshape(256, 256)


def solution(mesh):
    three, four = P("grp", "blk", None), P("grp", "blk", None, None)
    five = P("grp", "blk", None, None, None)
    return jax.shard_map(
        body,
        mesh=mesh,
        in_specs=(three, P(), three, five, three, five, three, three, four, three),
        out_specs=(three, three, P()),
        check_vma=False,
    )
```

time: 140 us -> 136 us (0.971)
  waiting for transfers between devices: 44.7 us -> 24.9 us
  starting transfers between devices: 71.1 us -> 83.1 us
  local copies, waits for them, and re-layouts: 3.99 us -> 6.53 us
  Pallas kernels: 16.5 us -> 18.2 us
    ppermute x7 -> x0, waiting for transfers between devices: 13.3 us -> none  [the longest x5 12.2 us: add_partner(): lax.ppermute(value, 'blk', [(i, i ^ 1 << step) for i in range(NX * NZ)])]
    all_to_all x1 -> x3, starting transfers between devices: 8.95 us -> 18.5 us  [the longest x1 10.5 us: body(): grad_weight = lax.all_to_all(shared, 'grp', 0, 0, tiled=True)]
    ppermute x7 -> x0, starting transfers between devices: 8.12 us -> none  [the longest x2 4.79 us: across_z(): return lax.ppermute(v, 'blk', [(i, i ^ 4) for i in range(NX * NZ)])]
    ppermute x18 -> x24, starting transfers between devices: 20.2 us -> 27.3 us  [go_x(): return lax.ppermute(v, 'blk', swap_x(kind))]
    all_to_all x1, waiting for transfers between devices: 6.72 us -> 0.01 us  [body(): lax.all_to_all(outgoing, 'grp', 0, 0, tiled=True).reshape(1024, 256)]
    all_to_all x1 -> x3, waiting for transfers between devices: 0.9 us -> 7.02 us  [the longest x2 4.61 us: add_group(): lax.all_to_all(jnp.broadcast_to(value[None], (n, 32, 256)), 'blk', 0, 0,...]
    ppermute x18 -> x24, waiting for transfers between devices: 11.8 us -> 7.35 us  [go_x(): return lax.ppermute(v, 'blk', swap_x(kind))]
    all_to_all x1, starting transfers between devices: 6.88 us -> 9.81 us  [body(): lax.all_to_all(outgoing, 'grp', 0, 0, tiled=True).reshape(1024, 256)]
  transfers between devices with their start and end apart: 40 -> 43, of which waited for: 18 -> 12; matrix products, arithmetic and copies ran while one was open for 3% -> 3% of each run, Pallas kernels for 8% -> 9%
where the time goes in v3:
time: 136 us; the launch traced here: 135 us
  starting transfers between devices  83.1 us (61%)
  waiting for transfers between devices  24.9 us (18%)
  Pallas kernels  18.2 us (13%)
  local copies, waits for them, and re-layouts  6.53 us (5%)
    ppermute x24, starting transfers between devices, go_x(): return lax.ppermute(v, 'blk', swap_x(kind))  27.3 us
    ppermute x14, starting transfers between devices, go_z(): return lax.ppermute(v, 'blk', swap_z(kind))  19.5 us
    pallas_call x5, Pallas kernels, call(): pl.pallas_call(kernel, out_shape=outs, in_specs=[HBM] * (len(ins) + len(p...  18.2 us
    all_to_all x1, starting transfers between devices, body(): grad_weight = lax.all_to_all(shared, 'grp', 0, 0, tiled=True)  10.5 us
    ppermute x14, waiting for transfers between devices, go_z(): return lax.ppermute(v, 'blk', swap_z(kind))  10.5 us
    all_to_all x1, starting transfers between devices, body(): lax.all_to_all(outgoing, 'grp', 0, 0, tiled=True).reshape(1024, 256)  9.81 us
    all_to_all x1, starting transfers between devices, body(): returned = lax.all_to_all(back, 'grp', 0, 0, tiled=True)  7.98 us
    all_to_all x2, starting transfers between devices, add_group(): lax.all_to_all(jnp.broadcast_to(value[None], (n, 32, 256)), 'blk', 0, 0,...  7.98 us
  transfers between devices with their start and end apart: 43, of which 12 were waited for; matrix products, arithmetic and copies ran while one was open for 3% of the time, Pallas kernels for 9%

profile of v3, /device:TPU:1, one launch (start us, length us, event | category | flops | bytes accessed | tf_op | source)
XLA Modules:
  0.0 134.8 jit_solution(12764196359003064995)
XLA Ops:
  0.6 2.6 %collective-permute-start.2 = (bf16[256,256]{1,0:T(8,128)(2,1)}, bf16[256,256]{1,0:T(8,128)(2,1)S(1)}, u32[]{:S(2)}, u32[]{:S(2)}) collective-permute-start(bf16[256,256]{1,0:T(8,128)(2,1)} %bitcast.23), channel_id=1, source_target_pairs={{0,8},{8,0},{16,24},{24,16},{32,40},{40,32},{48,56},{56,48},{64,72... | collective-permute-start | bytes 393224 | tf_op jit(solution)/shard_map/ppermute | solution.py:35
  3.2 4.7 %collective-permute-start = (bf16[256,256]{1,0:T(8,128)(2,1)}, bf16[256,256]{1,0:T(8,128)(2,1)S(1)}, u32[]{:S(2)}, u32[]{:S(2)}) collective-permute-start(bf16[256,256]{1,0:T(8,128)(2,1)} %bitcast.24), channel_id=1, source_target_pairs={{0,56},{8,16},{16,8},{24,32},{32,24},{40,48},{48,40},{56,0},{64,12... | collective-permute-start | bytes 393224 | tf_op jit(solution)/shard_map/ppermute | solution.py:35
  7.9 3.8 %collective-permute-start.3 = (bf16[256,256]{1,0:T(8,128)(2,1)S(1)}, bf16[256,256]{1,0:T(8,128)(2,1)S(1)}, u32[]{:S(2)}, u32[]{:S(2)}) collective-permute-start(bf16[256,256]{1,0:T(8,128)(2,1)S(1)} %collective-permute-done.2), channel_id=1, source_target_pairs={{0,56},{8,16},{16,8},{24,32},{32,24},{40,48},{48,40},{56,0},{64,12... | collective-permute-start | bytes 393224 | tf_op jit(solution)/shard_map/ppermute | solution.py:35
  12.6 2.6 %collective-permute-start.7 = (bf16[768,256]{1,0:T(8,128)(2,1)S(1)}, bf16[768,256]{1,0:T(8,128)(2,1)S(1)}, u32[]{:S(2)}, u32[]{:S(2)}) collective-permute-start(bf16[768,256]{1,0:T(8,128)(2,1)S(1)} %pad_maximum_fusion.refs_6_), channel_id=1, source_target_pairs={{0,192},{8,200},{16,208},{24,216},{32,224},{40,232},{48,240},{56,2... | collective-permute-start | bytes 1179656 | tf_op jit(solution)/shard_map/ppermute | solution.py:39
  24.6 2.3 %select.1 = (bf16[256,1024]{1,0:T(8,128)(2,1)}, bf16[8,128,256]{2,1,0:T(8,128)(2,1)}) custom-call(s32[8]{0:T(128)} %bitcast.34, s32[8,128]{1,0:T(8,128)} %bitcast.33, bf16[256,256]{1,0:T(8,128)(2,1)} %bitcast.26), custom_call_target="tpu_custom_call" | custom-call | flops 134217728 | bytes 1183776 | tf_op jit(solution)/shard_map/select/pallas_call | solution.py:226
  26.9 9.8 %all-to-all-start = ((bf16[8,128,256]{2,1,0:T(8,128)(2,1)}), bf16[8,128,256]{2,1,0:T(8,128)(2,1)S(1)}, u32[]{:S(2)}, u32[]{:S(2)}) async-start(bf16[8,128,256]{2,1,0:T(8,128)(2,1)} %get-tuple-element.24), calls=%async_computation | async-start | bytes 1048576 | tf_op jit(solution)/shard_map/all_to_all | solution.py:262
  38.5 3.7 %collective-permute-done.15.refs_18_ = bf16[256,256]{1,0:T(8,128)(2,1)S(1)} collective-permute-done((bf16[256,256]{1,0:T(8,128)(2,1)}, bf16[256,256]{1,0:T(8,128)(2,1)S(1)}, u32[]{:S(2)}, u32[]{:S(2)}) %collective-permute-start.15) | collective-permute-done | bytes 131104 | tf_op jit(solution)/shard_map/ppermute | solution.py:35
  47.6 3.1 %collective-permute-done.16.refs_19_ = bf16[256,256]{1,0:T(8,128)(2,1)} collective-permute-done((bf16[256,256]{1,0:T(8,128)(2,1)S(1)}, bf16[256,256]{1,0:T(8,128)(2,1)}, u32[]{:S(2)}, u32[]{:S(2)}) %collective-permute-start.16) | collective-permute-done | bytes 131104 | tf_op jit(solution)/shard_map/ppermute | solution.py:39
  53.3 3.0 %sparse.1 = (bf16[256,2048]{1,0:T(8,128)(2,1)}, f32[256,256]{1,0:T(8,128)}) custom-call(s32[32]{0:T(128)} %bitcast.30, s32[32]{0:T(128)} %bitcast.31, bf16[32,128,128]{2,1,0:T(8,128)(2,1)} %bitcast.18, bf16[1024,256]{1,0:T(8,128)(2,1)} %bitcast.17), custom_call_target="tpu_custom_call" | custom-call | flops 268435456 | bytes 2883840 | tf_op jit(solution)/shard_map/sparse/pallas_call | solution.py:226
  57.1 5.8 %forward.1 = (bf16[256,256]{1,0:T(8,128)(2,1)}, bf16[256,256]{1,0:T(8,128)(2,1)}, bf16[8,192,256]{2,1,0:T(8,128)(2,1)}) custom-call(s32[64]{0:T(128)} %bitcast.27, bf16[64,128,128]{2,1,0:T(8,128)(2,1)} %bitcast.14, bf16[256,2048]{1,0:T(8,128)(2,1)} %get-tuple-element.26.refs_2_, f32[256,256]{1,0:T(8,128)} %get-tuple-element.27.refs_3_, ...), custom_call_target="tpu_custom_call" | custom-call | flops 536870912 | bytes 4718848 | tf_op jit(solution)/shard_map/forward/pallas_call | solution.py:226
  64.7 8.0 %all-to-all-start.1 = ((bf16[8,192,256]{2,1,0:T(8,128)(2,1)}), bf16[8,192,256]{2,1,0:T(8,128)(2,1)S(1)}, u32[]{:S(2)}, u32[]{:S(2)}) async-start(bf16[8,192,256]{2,1,0:T(8,128)(2,1)} %get-tuple-element.35), calls=%async_computation.1 | async-start | bytes 1572864 | tf_op jit(solution)/shard_map/all_to_all | solution.py:310
  75.5 2.3 %collective-permute-done.23 = bf16[256,256]{1,0:T(8,128)(2,1)S(1)} collective-permute-done((bf16[256,256]{1,0:T(8,128)(2,1)S(1)}, bf16[256,256]{1,0:T(8,128)(2,1)S(1)}, u32[]{:S(2)}, u32[]{:S(2)}) %collective-permute-start.23) | collective-permute-done | bytes 131104 | tf_op jit(solution)/shard_map/ppermute | solution.py:35
  78.4 2.0 %collective-permute-start.22 = (bf16[768,256]{1,0:T(8,128)(2,1)S(1)}, bf16[768,256]{1,0:T(8,128)(2,1)S(1)}, u32[]{:S(2)}, u32[]{:S(2)}) collective-permute-start(bf16[768,256]{1,0:T(8,128)(2,1)S(1)} %constant_dynamic-update-slice_fusion.4.refs_2_), channel_id=1, source_target_pairs={{0,192},{8,200},{16,208},{24,216},{32,224},{40,232},{48,240},{56,2... | collective-permute-start | bytes 1179656 | tf_op jit(solution)/shard_map/ppermute | solution.py:39
  83.1 2.2 %collective-permute-start.26 = (bf16[512,256]{1,0:T(8,128)(2,1)S(1)}, bf16[512,256]{1,0:T(8,128)(2,1)}, u32[]{:S(2)}, u32[]{:S(2)}) collective-permute-start(bf16[512,256]{1,0:T(8,128)(2,1)S(1)} %constant_dynamic-update-slice_fusion.7.refs_5_), channel_id=1, source_target_pairs={{0,192},{8,200},{16,208},{24,216},{32,224},{40,232},{48,240},{56,2... | collective-permute-start | bytes 786440 | tf_op jit(solution)/shard_map/ppermute | solution.py:39
  87.9 1.9 %collective-permute-start.36 = (bf16[256,256]{1,0:T(8,128)(2,1)S(1)}, bf16[256,256]{1,0:T(8,128)(2,1)S(1)}, u32[]{:S(2)}, u32[]{:S(2)}) collective-permute-start(bf16[256,256]{1,0:T(8,128)(2,1)S(1)} %collective-permute-done.28.refs_8_), channel_id=1, source_target_pairs={{0,192},{8,200},{16,208},{24,216},{32,224},{40,232},{48,240},{56,2... | collective-permute-start | bytes 393224 | tf_op jit(solution)/shard_map/ppermute | solution.py:39
  90.9 3.3 %all-to-all-start.2 = ((f32[4,32,256]{2,1,0:T(8,128)}), f32[4,32,256]{2,1,0:T(8,128)S(1)}, u32[]{:S(2)}, u32[]{:S(2)}) async-start(f32[4,32,256]{2,1,0:T(8,128)} %broadcast_in_dim.12), calls=%async_computation.2 | async-start | bytes 262144 | tf_op jit(solution)/shard_map/all_to_all | solution.py:316
  94.3 2.8 %collective-permute-start.33 = (bf16[512,256]{1,0:T(8,128)(2,1)S(1)}, bf16[512,256]{1,0:T(8,128)(2,1)}, u32[]{:S(2)}, u32[]{:S(2)}) collective-permute-start(bf16[512,256]{1,0:T(8,128)(2,1)S(1)} %constant_dynamic-update-slice_fusion.9.refs_8_), channel_id=1, source_target_pairs={{0,192},{8,200},{16,208},{24,216},{32,224},{40,232},{48,240},{56,2... | collective-permute-start | bytes 786440 | tf_op jit(solution)/shard_map/ppermute | solution.py:39
  97.7 2.1 %all-to-all-done.2 = f32[4,32,256]{2,1,0:T(8,128)S(1)} async-done(((f32[4,32,256]{2,1,0:T(8,128)}), f32[4,32,256]{2,1,0:T(8,128)S(1)}, u32[]{:S(2)}, u32[]{:S(2)}) %all-to-all-start.2) | async-done | bytes 131104 | tf_op jit(solution)/shard_map/all_to_all | solution.py:316
  100.7 4.6 %all-to-all-start.3 = ((f32[8,32,256]{2,1,0:T(8,128)}), f32[8,32,256]{2,1,0:T(8,128)S(1)}, u32[]{:S(2)}, u32[]{:S(2)}) async-start(f32[8,32,256]{2,1,0:T(8,128)} %broadcast_in_dim.13), calls=%async_computation.3 | async-start | bytes 524288 | tf_op jit(solution)/shard_map/all_to_all | solution.py:316
  109.0 3.2 %early.1.refs_2_ = f32[256,256]{1,0:T(8,128)} custom-call(s32[64]{0:T(128)} %bitcast.28, bf16[64,128,128]{2,1,0:T(8,128)(2,1)} %bitcast.15, bf16[768,256]{1,0:T(8,128)(2,1)} %copy-done.3, bf16[768,256]{1,0:T(8,128)(2,1)} %copy-done.12, bf16[768,256]{1,0:T(8,128)(2,1)} %copy-done.11, bf16[512,256]{1,0:T(8,128)(2,1)} %copy-done.5, ...), custom_call_target="tpu_custom_call" | custom-call | flops 268435456 | bytes 2359552 | tf_op jit(solution)/shard_map/early/pallas_call | solution.py:226
  112.2 2.5 %all-to-all-done.3 = f32[8,32,256]{2,1,0:T(8,128)S(1)} async-done(((f32[8,32,256]{2,1,0:T(8,128)}), f32[8,32,256]{2,1,0:T(8,128)S(1)}, u32[]{:S(2)}, u32[]{:S(2)}) %all-to-all-start.3) | async-done | bytes 262176 | tf_op jit(solution)/shard_map/all_to_all | solution.py:316
  117.1 10.5 %all-to-all-start.4 = ((f32[8,32,256]{2,1,0:T(8,128)}), f32[8,32,256]{2,1,0:T(8,128)S(1)}, u32[]{:S(2)}, u32[]{:S(2)}) async-start(f32[8,32,256]{2,1,0:T(8,128)} %broadcast_in_dim.28), calls=%async_computation.4 | async-start | bytes 524288 | tf_op jit(solution)/shard_map/all_to_all | solution.py:338
  127.6 4.1 %backward.1 = bf16[256,256]{1,0:T(8,128)(2,1)} custom-call(s32[64]{0:T(128)} %bitcast.29, bf16[64,128,128]{2,1,0:T(8,128)(2,1)} %bitcast.16, f32[256,256]{1,0:T(8,128)} %early.1.refs_2_, bf16[256,1024]{1,0:T(8,128)(2,1)} %get-tuple-element.34.refs_3_, bf16[8,192,256]{2,1,0:T(8,128)(2,1)} %copy-done, bf16[256,256]{1,0:T(8,128)(2,1)} %refs_5_.1, ...), custom_call_target="tpu_custom_call" | custom-call | flops 268435456 | bytes 3932416 | tf_op jit(solution)/shard_map/backward/pallas_call | solution.py:226
  131.7 2.4 %all-to-all-done.4 = f32[8,32,256]{2,1,0:T(8,128)S(1)} async-done(((f32[8,32,256]{2,1,0:T(8,128)}), f32[8,32,256]{2,1,0:T(8,128)S(1)}, u32[]{:S(2)}, u32[]{:S(2)}) %all-to-all-start.4) | async-done | bytes 262176 | tf_op jit(solution)/shard_map/all_to_all | solution.py:338
  (133 shorter events, 40.6 us)
Async XLA Ops:
  12.6 12.0 %collective-permute-start.7 = (bf16[768,256]{1,0:T(8,128)(2,1)S(1)}, bf16[768,256]{1,0:T(8,128)(2,1)S(1)}, u32[]{:S(2)}, u32[]{:S(2)}) collective-permute-start(bf16[768,256]{1,0:T(8,128)(2,1)S(1)} %pad_maximum_fusion.refs_6_), channel_id=1, source_target_pairs={{0,192},{8,200},{16,208},{24,216},{32,224},{40,232},{48,240},{56,2... | collective-permute-start | bytes 1179656 | tf_op jit(solution)/shard_map/ppermute | solution.py:39
  15.2 21.5 %collective-permute-start.6 = (bf16[768,256]{1,0:T(8,128)(2,1)S(1)}, bf16[768,256]{1,0:T(8,128)(2,1)S(1)}, u32[]{:S(2)}, u32[]{:S(2)}) collective-permute-start(bf16[768,256]{1,0:T(8,128)(2,1)S(1)} %pad_maximum_fusion.refs_6_), channel_id=1, source_target_pairs={{0,64},{8,72},{16,80},{24,88},{32,96},{40,104},{48,112},{56,120},{... | collective-permute-start | bytes 1179656 | tf_op jit(solution)/shard_map/ppermute | solution.py:39
  18.1 18.7 %collective-permute-start.5 = (bf16[512,256]{1,0:T(8,128)(2,1)S(1)}, bf16[512,256]{1,0:T(8,128)(2,1)S(1)}, u32[]{:S(2)}, u32[]{:S(2)}) collective-permute-start(bf16[512,256]{1,0:T(8,128)(2,1)S(1)} %constant_dynamic-update-slice_fusion.refs_10_), channel_id=1, source_target_pairs={{0,192},{8,200},{16,208},{24,216},{32,224},{40,232},{48,240},{56,2... | collective-permute-start | bytes 786440 | tf_op jit(solution)/shard_map/ppermute | solution.py:39
  19.5 18.9 %collective-permute-start.4 = (bf16[512,256]{1,0:T(8,128)(2,1)S(1)}, bf16[512,256]{1,0:T(8,128)(2,1)S(1)}, u32[]{:S(2)}, u32[]{:S(2)}) collective-permute-start(bf16[512,256]{1,0:T(8,128)(2,1)S(1)} %constant_dynamic-update-slice_fusion.refs_10_), channel_id=1, source_target_pairs={{0,64},{8,72},{16,80},{24,88},{32,96},{40,104},{48,112},{56,120},{... | collective-permute-start | bytes 786440 | tf_op jit(solution)/shard_map/ppermute | solution.py:39
  22.9 21.0 %collective-permute-start.13 = (bf16[512,256]{1,0:T(8,128)(2,1)S(1)}, bf16[512,256]{1,0:T(8,128)(2,1)S(1)}, u32[]{:S(2)}, u32[]{:S(2)}) collective-permute-start(bf16[512,256]{1,0:T(8,128)(2,1)S(1)} %constant_dynamic-update-slice_fusion.2.refs_14_), channel_id=1, source_target_pairs={{0,192},{8,200},{16,208},{24,216},{32,224},{40,232},{48,240},{56,2... | collective-permute-start | bytes 786440 | tf_op jit(solution)/shard_map/ppermute | solution.py:39
  24.6 21.1 %collective-permute-start.12 = (bf16[512,256]{1,0:T(8,128)(2,1)S(1)}, bf16[512,256]{1,0:T(8,128)(2,1)}, u32[]{:S(2)}, u32[]{:S(2)}) collective-permute-start(bf16[512,256]{1,0:T(8,128)(2,1)S(1)} %constant_dynamic-update-slice_fusion.2.refs_14_), channel_id=1, source_target_pairs={{0,64},{8,72},{16,80},{24,88},{32,96},{40,104},{48,112},{56,120},{... | collective-permute-start | bytes 786440 | tf_op jit(solution)/shard_map/ppermute | solution.py:39
  26.9 25.6 %all-to-all-start = ((bf16[8,128,256]{2,1,0:T(8,128)(2,1)}), bf16[8,128,256]{2,1,0:T(8,128)(2,1)S(1)}, u32[]{:S(2)}, u32[]{:S(2)}) async-start(bf16[8,128,256]{2,1,0:T(8,128)(2,1)} %get-tuple-element.24), calls=%async_computation | async-start | bytes 1048576 | tf_op jit(solution)/shard_map/all_to_all | solution.py:262
  36.8 19.5 %collective-permute-start.8 = (bf16[768,256]{1,0:T(8,128)(2,1)S(1)}, bf16[768,256]{1,0:T(8,128)(2,1)S(1)}, u32[]{:S(2)}, u32[]{:S(2)}) collective-permute-start(bf16[768,256]{1,0:T(8,128)(2,1)S(1)} %collective-permute-done.7.refs_8_), channel_id=1, source_target_pairs={{0,64},{8,72},{16,80},{24,88},{32,96},{40,104},{48,112},{56,120},{... | collective-permute-start | bytes 1179656 | tf_op jit(solution)/shard_map/ppermute | solution.py:39
  44.0 12.3 %collective-permute-start.9 = (bf16[512,256]{1,0:T(8,128)(2,1)S(1)}, bf16[512,256]{1,0:T(8,128)(2,1)}, u32[]{:S(2)}, u32[]{:S(2)}) collective-permute-start(bf16[512,256]{1,0:T(8,128)(2,1)S(1)} %collective-permute-done.4.refs_11_), channel_id=1, source_target_pairs={{0,192},{8,200},{16,208},{24,216},{32,224},{40,232},{48,240},{56,2... | collective-permute-start | bytes 786440 | tf_op jit(solution)/shard_map/ppermute | solution.py:39
  45.7 10.6 %collective-permute-start.14 = (bf16[512,256]{1,0:T(8,128)(2,1)S(1)}, bf16[512,256]{1,0:T(8,128)(2,1)}, u32[]{:S(2)}, u32[]{:S(2)}) collective-permute-start(bf16[512,256]{1,0:T(8,128)(2,1)S(1)} %collective-permute-done.13.refs_16_), channel_id=1, source_target_pairs={{0,64},{8,72},{16,80},{24,88},{32,96},{40,104},{48,112},{56,120},{... | collective-permute-start | bytes 786440 | tf_op jit(solution)/shard_map/ppermute | solution.py:39
  62.9 9.8 %collective-permute-start.20 = (bf16[256,256]{1,0:T(8,128)(2,1)}, bf16[256,256]{1,0:T(8,128)(2,1)S(1)}, u32[]{:S(2)}, u32[]{:S(2)}) collective-permute-start(bf16[256,256]{1,0:T(8,128)(2,1)} %get-tuple-element.33), channel_id=1, source_target_pairs={{0,56},{8,16},{16,8},{24,32},{32,24},{40,48},{48,40},{56,0},{64,12... | collective-permute-start | bytes 393224 | tf_op jit(solution)/shard_map/ppermute | solution.py:35
  64.6 9.7 %collective-permute-start.19 = (bf16[256,256]{1,0:T(8,128)(2,1)}, bf16[256,256]{1,0:T(8,128)(2,1)S(1)}, u32[]{:S(2)}, u32[]{:S(2)}) collective-permute-start(bf16[256,256]{1,0:T(8,128)(2,1)} %get-tuple-element.33), channel_id=1, source_target_pairs={{0,8},{8,0},{16,24},{24,16},{32,40},{40,32},{48,56},{56,48},{64,72... | collective-permute-start | bytes 393224 | tf_op jit(solution)/shard_map/ppermute | solution.py:35
  64.7 25.1 %all-to-all-start.1 = ((bf16[8,192,256]{2,1,0:T(8,128)(2,1)}), bf16[8,192,256]{2,1,0:T(8,128)(2,1)S(1)}, u32[]{:S(2)}, u32[]{:S(2)}) async-start(bf16[8,192,256]{2,1,0:T(8,128)(2,1)} %get-tuple-element.35), calls=%async_computation.1 | async-start | bytes 1572864 | tf_op jit(solution)/shard_map/all_to_all | solution.py:310
  78.4 11.4 %collective-permute-start.22 = (bf16[768,256]{1,0:T(8,128)(2,1)S(1)}, bf16[768,256]{1,0:T(8,128)(2,1)S(1)}, u32[]{:S(2)}, u32[]{:S(2)}) collective-permute-start(bf16[768,256]{1,0:T(8,128)(2,1)S(1)} %constant_dynamic-update-slice_fusion.4.refs_2_), channel_id=1, source_target_pairs={{0,192},{8,200},{16,208},{24,216},{32,224},{40,232},{48,240},{56,2... | collective-permute-start | bytes 1179656 | tf_op jit(solution)/shard_map/ppermute | solution.py:39
  80.4 9.6 %collective-permute-start.21 = (bf16[768,256]{1,0:T(8,128)(2,1)S(1)}, bf16[768,256]{1,0:T(8,128)(2,1)S(1)}, u32[]{:S(2)}, u32[]{:S(2)}) collective-permute-start(bf16[768,256]{1,0:T(8,128)(2,1)S(1)} %constant_dynamic-update-slice_fusion.4.refs_2_), channel_id=1, source_target_pairs={{0,64},{8,72},{16,80},{24,88},{32,96},{40,104},{48,112},{56,120},{... | collective-permute-start | bytes 1179656 | tf_op jit(solution)/shard_map/ppermute | solution.py:39
  83.1 22.5 %collective-permute-start.26 = (bf16[512,256]{1,0:T(8,128)(2,1)S(1)}, bf16[512,256]{1,0:T(8,128)(2,1)}, u32[]{:S(2)}, u32[]{:S(2)}) collective-permute-start(bf16[512,256]{1,0:T(8,128)(2,1)S(1)} %constant_dynamic-update-slice_fusion.7.refs_5_), channel_id=1, source_target_pairs={{0,192},{8,200},{16,208},{24,216},{32,224},{40,232},{48,240},{56,2... | collective-permute-start | bytes 786440 | tf_op jit(solution)/shard_map/ppermute | solution.py:39
  85.3 20.3 %collective-permute-start.25 = (bf16[512,256]{1,0:T(8,128)(2,1)S(1)}, bf16[512,256]{1,0:T(8,128)(2,1)S(1)}, u32[]{:S(2)}, u32[]{:S(2)}) collective-permute-start(bf16[512,256]{1,0:T(8,128)(2,1)S(1)} %constant_dynamic-update-slice_fusion.7.refs_5_), channel_id=1, source_target_pairs={{0,64},{8,72},{16,80},{24,88},{32,96},{40,104},{48,112},{56,120},{... | collective-permute-start | bytes 786440 | tf_op jit(solution)/shard_map/ppermute | solution.py:39
  87.9 9.8 %collective-permute-start.36 = (bf16[256,256]{1,0:T(8,128)(2,1)S(1)}, bf16[256,256]{1,0:T(8,128)(2,1)S(1)}, u32[]{:S(2)}, u32[]{:S(2)}) collective-permute-start(bf16[256,256]{1,0:T(8,128)(2,1)S(1)} %collective-permute-done.28.refs_8_), channel_id=1, source_target_pairs={{0,192},{8,200},{16,208},{24,216},{32,224},{40,232},{48,240},{56,2... | collective-permute-start | bytes 393224 | tf_op jit(solution)/shard_map/ppermute | solution.py:39
  89.9 10.0 %collective-permute-start.35 = (bf16[256,256]{1,0:T(8,128)(2,1)S(1)}, bf16[256,256]{1,0:T(8,128)(2,1)S(1)}, u32[]{:S(2)}, u32[]{:S(2)}) collective-permute-start(bf16[256,256]{1,0:T(8,128)(2,1)S(1)} %collective-permute-done.28.refs_8_), channel_id=1, source_target_pairs={{0,64},{8,72},{16,80},{24,88},{32,96},{40,104},{48,112},{56,120},{... | collective-permute-start | bytes 393224 | tf_op jit(solution)/shard_map/ppermute | solution.py:39
  94.3 12.8 %collective-permute-start.33 = (bf16[512,256]{1,0:T(8,128)(2,1)S(1)}, bf16[512,256]{1,0:T(8,128)(2,1)}, u32[]{:S(2)}, u32[]{:S(2)}) collective-permute-start(bf16[512,256]{1,0:T(8,128)(2,1)S(1)} %constant_dynamic-update-slice_fusion.9.refs_8_), channel_id=1, source_target_pairs={{0,192},{8,200},{16,208},{24,216},{32,224},{40,232},{48,240},{56,2... | collective-permute-start | bytes 786440 | tf_op jit(solution)/shard_map/ppermute | solution.py:39
  97.7 9.4 %collective-permute-start.32 = (bf16[512,256]{1,0:T(8,128)(2,1)S(1)}, bf16[512,256]{1,0:T(8,128)(2,1)}, u32[]{:S(2)}, u32[]{:S(2)}) collective-permute-start(bf16[512,256]{1,0:T(8,128)(2,1)S(1)} %constant_dynamic-update-slice_fusion.9.refs_8_), channel_id=1, source_target_pairs={{0,64},{8,72},{16,80},{24,88},{32,96},{40,104},{48,112},{56,120},{... | collective-permute-start | bytes 786440 | tf_op jit(solution)/shard_map/ppermute | solution.py:39
  100.7 14.0 %all-to-all-start.3 = ((f32[8,32,256]{2,1,0:T(8,128)}), f32[8,32,256]{2,1,0:T(8,128)S(1)}, u32[]{:S(2)}, u32[]{:S(2)}) async-start(f32[8,32,256]{2,1,0:T(8,128)} %broadcast_in_dim.13), calls=%async_computation.3 | async-start | bytes 524288 | tf_op jit(solution)/shard_map/all_to_all | solution.py:316
  105.3 9.4 %collective-permute-start.29 = (bf16[768,256]{1,0:T(8,128)(2,1)S(1)}, bf16[768,256]{1,0:T(8,128)(2,1)S(1)}, u32[]{:S(2)}, u32[]{:S(2)}) collective-permute-start(bf16[768,256]{1,0:T(8,128)(2,1)S(1)} %collective-permute-done.22.refs_4_), channel_id=1, source_target_pairs={{0,64},{8,72},{16,80},{24,88},{32,96},{40,104},{48,112},{56,120},{... | collective-permute-start | bytes 1179656 | tf_op jit(solution)/shard_map/ppermute | solution.py:39
  117.1 17.0 %all-to-all-start.4 = ((f32[8,32,256]{2,1,0:T(8,128)}), f32[8,32,256]{2,1,0:T(8,128)S(1)}, u32[]{:S(2)}, u32[]{:S(2)}) async-start(f32[8,32,256]{2,1,0:T(8,128)} %broadcast_in_dim.28), calls=%async_computation.4 | async-start | bytes 524288 | tf_op jit(solution)/shard_map/all_to_all | solution.py:338
  (42 other events, 536.6 us)

commit v4 on v3

--- a/solution.py
+++ b/solution.py
@@ -121,7 +121,6 @@
 
 
 EARLY = (0, 1, 2, 4, 5, 6, 12)
-ALL = tuple(range(16))
 LATE = (3, 7, 8, 9, 10, 11, 13, 14, 15)
 
 
@@ -172,19 +171,19 @@
 
 
 def forward_kernel(*refs):
-    n = len(ALL)
-    cols_any, tiles_any, s_any, sum_any, w_any, cot_any = refs[:6]
-    hidden_ref, grad_ref, back_ref = refs[6 + n : 9 + n]
-    s_ref, sum_ref, w_ref, cot_ref, sems, cols_ref, tiles_ref, tile_sems, piece_sems = refs[9 + n : 18 + n]
-    ins = [(cols_any, cols_ref), (sum_any, sum_ref), (w_any, w_ref), (cot_any, cot_ref)]
+    n = len(LATE)
+    cols_any, tiles_any, early_any, s_any, sum_any, w_any, cot_any = refs[:7]
+    hidden_ref, grad_ref, back_ref = refs[7 + n : 10 + n]
+    early_ref, s_ref, sum_ref, w_ref, cot_ref, sems, cols_ref, tiles_ref, tile_sems, piece_sems = refs[10 + n : 20 + n]
+    ins = [(cols_any, cols_ref), (early_any, early_ref), (sum_any, sum_ref), (w_any, w_ref), (cot_any, cot_ref)]
     copies = load(ins + [(s_any, s_ref)], sems)
     agg = dense_product(
-        ALL, cols_ref, copies[0], tiles_any, tiles_ref, tile_sems, refs[6 : 6 + n], refs[-n:], piece_sems
+        LATE, cols_ref, copies[0], tiles_any, tiles_ref, tile_sems, refs[7 : 7 + n], refs[-n:], piece_sems
     )
     for c in copies[1:]:
         c.wait()
     half = 8 * TILE
-    high, low = split(agg + sum_ref[...])
+    high, low = split(agg + early_ref[...] + sum_ref[...])
     pre = dot(high, w_ref[...]) + dot(low, w_ref[...])
     sig = jax.nn.sigmoid(pre)
     hidden_ref[...] = (pre * sig).astype(BF)
@@ -272,6 +271,10 @@
         if i == SELECT_AT:
 
             held.extend([sel, received])
+        if i == 6:
+            sums.append(early(values))
+        if i == 8:
+            return tie(values, sums[0])
         if i == 4:
             rec = tie(held[1], values)
             held.extend(
@@ -296,16 +299,17 @@
     pieces = gather(own, forward_hook)
     sel, _, sparse, sparse_sum = held
 
+    taken = [pieces[i] for i in LATE]
     hidden, grad, back = call(
         forward_kernel,
-        [ints, tiles, sparse, sparse_sum, weight, cotangent[0]],
+        [ints, tiles, sums[0], sparse, sparse_sum, weight, cotangent[0]],
         [shape(square, BF), shape(square, BF), shape((8, TILE + 64, 256), BF)],
-        [pltpu.VMEM((256, 2048), BF), pltpu.VMEM(square, F32), pltpu.VMEM(square, BF)]
-        + [pltpu.VMEM(square, BF), DMA((5,))]
-        + dense_scratch(pieces),
+        [pltpu.VMEM(square, F32), pltpu.VMEM((256, 2048), BF), pltpu.VMEM(square, F32), pltpu.VMEM(square, BF)]
+        + [pltpu.VMEM(square, BF), DMA((6,))]
+        + dense_scratch(taken),
         "forward",
         2 * 256 * 4096 * 256,
-        pieces,
+        taken,
     )
     returned = lax.all_to_all(back, "grp", 0, 0, tiled=True)
     part = []
@@ -328,7 +332,7 @@
         if i == 8:
             add_group([[x * NZ + z for z in range(NZ)] for x in range(NX)], values)
         if i == 9:
-            part.append(tie(part[-1], values, sums[0]))
+            part.append(tie(part[-1], values, sums[1]))
         if i in (10, 11):
             part.append(tie(part[-1], values))
         return values
@@ -339,7 +343,7 @@
     taken = [grad_pieces[i] for i in LATE]
     grad_features = call(
         backward_kernel,
-        [ints, tiles, sums[0], sel, returned, weight],
+        [ints, tiles, sums[1], sel, returned, weight],
         shape(square, BF),
         [pltpu.VMEM(square, F32), pltpu.VMEM((256, 1024), BF), pltpu.VMEM((8, TILE, 256), BF), pltpu.VMEM(square, BF)]
         + [DMA((5,))]

time: 136 us -> 135 us (level)
  starting transfers between devices: 83.1 us -> 74.8 us
  waiting for transfers between devices: 24.9 us -> 30.3 us
  Pallas kernels: 18.2 us -> 20.3 us
    ppermute x24, starting transfers between devices: 27.3 us -> 18.3 us  [go_x(): return lax.ppermute(v, 'blk', swap_x(kind))]
    ppermute x14, waiting for transfers between devices: 10.5 us -> 14.7 us  [go_z(): return lax.ppermute(v, 'blk', swap_z(kind))]
    pallas_call x5 -> x6, Pallas kernels: 18.2 us -> 20.3 us  [call(): pl.pallas_call(kernel, out_shape=outs, in_specs=[HBM] * (len(ins) + len(p...]
    ppermute x24, waiting for transfers between devices: 7.35 us -> 9.16 us  [go_x(): return lax.ppermute(v, 'blk', swap_x(kind))]
    ppermute x14, starting transfers between devices: 19.5 us -> 20.9 us  [go_z(): return lax.ppermute(v, 'blk', swap_z(kind))]
    unnamed x53 -> x57, local copies, waits for them, and re-layouts: 3.2 us -> 4.09 us
  transfers between devices with their start and end apart: 43 -> 43, of which waited for: 12 -> 17; matrix products, arithmetic and copies ran while one was open for 3% -> 3% of each run, Pallas kernels for 9% -> 12%
where the time goes in v4:
time: 135 us; the launch traced here: 134 us
  starting transfers between devices  74.8 us (55%)
  waiting for transfers between devices  30.3 us (22%)
  Pallas kernels  20.3 us (15%)
  local copies, waits for them, and re-layouts  6.35 us (5%)
    ppermute x14, starting transfers between devices, go_z(): return lax.ppermute(v, 'blk', swap_z(kind))  20.9 us
    pallas_call x6, Pallas kernels, call(): pl.pallas_call(kernel, out_shape=outs, in_specs=[HBM] * (len(ins) + len(p...  20.3 us
    ppermute x24, starting transfers between devices, go_x(): return lax.ppermute(v, 'blk', swap_x(kind))  18.3 us
    ppermute x14, waiting for transfers between devices, go_z(): return lax.ppermute(v, 'blk', swap_z(kind))  14.7 us
    all_to_all x1, starting transfers between devices, body(): lax.all_to_all(outgoing, 'grp', 0, 0, tiled=True).reshape(1024, 256)  10.2 us
    all_to_all x1, starting transfers between devices, body(): grad_weight = lax.all_to_all(shared, 'grp', 0, 0, tiled=True)  9.65 us
    ppermute x24, waiting for transfers between devices, go_x(): return lax.ppermute(v, 'blk', swap_x(kind))  9.16 us
    all_to_all x1, starting transfers between devices, body(): returned = lax.all_to_all(back, 'grp', 0, 0, tiled=True)  7.99 us
  transfers between devices with their start and end apart: 43, of which 17 were waited for; matrix products, arithmetic and copies ran while one was open for 3% of the time, Pallas kernels for 12%

profile of v4, /device:TPU:1, one launch (start us, length us, event | category | flops | bytes accessed | tf_op | source)
XLA Modules:
  0.0 133.8 jit_solution(15289618020891586174)
XLA Ops:
  0.6 2.6 %collective-permute-start = (bf16[256,256]{1,0:T(8,128)(2,1)}, bf16[256,256]{1,0:T(8,128)(2,1)S(1)}, u32[]{:S(2)}, u32[]{:S(2)}) collective-permute-start(bf16[256,256]{1,0:T(8,128)(2,1)} %bitcast.24), channel_id=1, source_target_pairs={{0,8},{8,0},{16,24},{24,16},{32,40},{40,32},{48,56},{56,48},{64,72... | collective-permute-start | bytes 393224 | tf_op jit(solution)/shard_map/ppermute | solution.py:35
  3.2 4.7 %collective-permute-start.1 = (bf16[256,256]{1,0:T(8,128)(2,1)}, bf16[256,256]{1,0:T(8,128)(2,1)S(1)}, u32[]{:S(2)}, u32[]{:S(2)}) collective-permute-start(bf16[256,256]{1,0:T(8,128)(2,1)} %bitcast.25), channel_id=1, source_target_pairs={{0,56},{8,16},{16,8},{24,32},{32,24},{40,48},{48,40},{56,0},{64,12... | collective-permute-start | bytes 393224 | tf_op jit(solution)/shard_map/ppermute | solution.py:35
  7.9 3.8 %collective-permute-start.5 = (bf16[256,256]{1,0:T(8,128)(2,1)S(1)}, bf16[256,256]{1,0:T(8,128)(2,1)S(1)}, u32[]{:S(2)}, u32[]{:S(2)}) collective-permute-start(bf16[256,256]{1,0:T(8,128)(2,1)S(1)} %collective-permute-done), channel_id=1, source_target_pairs={{0,56},{8,16},{16,8},{24,32},{32,24},{40,48},{48,40},{56,0},{64,12... | collective-permute-start | bytes 393224 | tf_op jit(solution)/shard_map/ppermute | solution.py:35
  13.9 1.8 %collective-permute-start.3 = (bf16[768,256]{1,0:T(8,128)(2,1)S(1)}, bf16[768,256]{1,0:T(8,128)(2,1)S(1)}, u32[]{:S(2)}, u32[]{:S(2)}) collective-permute-start(bf16[768,256]{1,0:T(8,128)(2,1)S(1)} %pad_maximum_fusion.refs_2_), channel_id=1, source_target_pairs={{0,192},{8,200},{16,208},{24,216},{32,224},{40,232},{48,240},{56,2... | collective-permute-start | bytes 1179656 | tf_op jit(solution)/shard_map/ppermute | solution.py:39
  19.9 2.1 %collective-permute-start.7 = (bf16[512,256]{1,0:T(8,128)(2,1)S(1)}, bf16[512,256]{1,0:T(8,128)(2,1)}, u32[]{:S(2)}, u32[]{:S(2)}) collective-permute-start(bf16[512,256]{1,0:T(8,128)(2,1)S(1)} %constant_dynamic-update-slice_fusion.refs_5_), channel_id=1, source_target_pairs={{0,192},{8,200},{16,208},{24,216},{32,224},{40,232},{48,240},{56,2... | collective-permute-start | bytes 786440 | tf_op jit(solution)/shard_map/ppermute | solution.py:39
  24.1 2.1 %select.1 = (bf16[256,1024]{1,0:T(8,128)(2,1)}, bf16[8,128,256]{2,1,0:T(8,128)(2,1)}) custom-call(s32[8]{0:T(128)} %bitcast.36, s32[8,128]{1,0:T(8,128)} %bitcast.35, bf16[256,256]{1,0:T(8,128)(2,1)} %bitcast.27), custom_call_target="tpu_custom_call" | custom-call | flops 134217728 | bytes 1183776 | tf_op jit(solution)/shard_map/select/pallas_call | solution.py:225
  26.2 10.2 %all-to-all-start = ((bf16[8,128,256]{2,1,0:T(8,128)(2,1)}), bf16[8,128,256]{2,1,0:T(8,128)(2,1)S(1)}, u32[]{:S(2)}, u32[]{:S(2)}) async-start(bf16[8,128,256]{2,1,0:T(8,128)(2,1)} %get-tuple-element.26), calls=%async_computation | async-start | bytes 1048576 | tf_op jit(solution)/shard_map/all_to_all | solution.py:261
  37.8 3.8 %collective-permute-done.9.refs_8_ = bf16[256,256]{1,0:T(8,128)(2,1)S(1)} collective-permute-done((bf16[256,256]{1,0:T(8,128)(2,1)S(1)}, bf16[256,256]{1,0:T(8,128)(2,1)S(1)}, u32[]{:S(2)}, u32[]{:S(2)}) %collective-permute-start.9) | collective-permute-done | bytes 131104 | tf_op jit(solution)/shard_map/ppermute | solution.py:35
  42.5 2.0 %collective-permute-start.11 = (bf16[512,256]{1,0:T(8,128)(2,1)S(1)}, bf16[512,256]{1,0:T(8,128)(2,1)}, u32[]{:S(2)}, u32[]{:S(2)}) collective-permute-start(bf16[512,256]{1,0:T(8,128)(2,1)S(1)} %collective-permute-done.6.refs_6_), channel_id=1, source_target_pairs={{0,192},{8,200},{16,208},{24,216},{32,224},{40,232},{48,240},{56,2... | collective-permute-start | bytes 786440 | tf_op jit(solution)/shard_map/ppermute | solution.py:39
  44.6 3.2 %early.2.refs_2_ = f32[256,256]{1,0:T(8,128)} custom-call(s32[64]{0:T(128)} %bitcast.28, bf16[64,128,128]{2,1,0:T(8,128)(2,1)} %bitcast.14, bf16[768,256]{1,0:T(8,128)(2,1)} %copy-done.2, bf16[768,256]{1,0:T(8,128)(2,1)} %copy-done.11, bf16[768,256]{1,0:T(8,128)(2,1)} %copy-done.9, bf16[512,256]{1,0:T(8,128)(2,1)} %copy-done.7, bf16[512,256]{1,0:T(8,128)(2,1)} %copy-done.15, ...), custom_call_target="tpu_custom_call" | custom-call | flops 268435456 | bytes 2359552 | tf_op jit(solution)/shard_map/early/pallas_call | solution.py:225
  47.8 3.3 %collective-permute-done.16.refs_13_ = bf16[256,256]{1,0:T(8,128)(2,1)S(1)} collective-permute-done((bf16[256,256]{1,0:T(8,128)(2,1)S(1)}, bf16[256,256]{1,0:T(8,128)(2,1)S(1)}, u32[]{:S(2)}, u32[]{:S(2)}) %collective-permute-start.16) | collective-permute-done | bytes 131104 | tf_op jit(solution)/shard_map/ppermute | solution.py:39
  52.9 3.0 %sparse.1 = (bf16[256,2048]{1,0:T(8,128)(2,1)}, f32[256,256]{1,0:T(8,128)}) custom-call(s32[32]{0:T(128)} %bitcast.32, s32[32]{0:T(128)} %bitcast.33, bf16[32,128,128]{2,1,0:T(8,128)(2,1)} %bitcast.19, bf16[1024,256]{1,0:T(8,128)(2,1)} %bitcast.18), custom_call_target="tpu_custom_call" | custom-call | flops 268435456 | bytes 2883840 | tf_op jit(solution)/shard_map/sparse/pallas_call | solution.py:225
  57.8 4.8 %forward.1 = (bf16[256,256]{1,0:T(8,128)(2,1)}, bf16[256,256]{1,0:T(8,128)(2,1)}, bf16[8,192,256]{2,1,0:T(8,128)(2,1)}) custom-call(s32[64]{0:T(128)} %bitcast.29, bf16[64,128,128]{2,1,0:T(8,128)(2,1)} %bitcast.15, f32[256,256]{1,0:T(8,128)} %early.2.refs_2_, bf16[256,2048]{1,0:T(8,128)(2,1)} %get-tuple-element.28.refs_3_, ...), custom_call_target="tpu_custom_call" | custom-call | flops 536870912 | bytes 4980992 | tf_op jit(solution)/shard_map/forward/pallas_call | solution.py:225
  64.3 8.0 %all-to-all-start.1 = ((bf16[8,192,256]{2,1,0:T(8,128)(2,1)}), bf16[8,192,256]{2,1,0:T(8,128)(2,1)S(1)}, u32[]{:S(2)}, u32[]{:S(2)}) async-start(bf16[8,192,256]{2,1,0:T(8,128)(2,1)} %get-tuple-element.39), calls=%async_computation.1 | async-start | bytes 1572864 | tf_op jit(solution)/shard_map/all_to_all | solution.py:314
  81.0 2.5 %collective-permute-done.27 = bf16[256,256]{1,0:T(8,128)(2,1)S(1)} collective-permute-done((bf16[256,256]{1,0:T(8,128)(2,1)S(1)}, bf16[256,256]{1,0:T(8,128)(2,1)S(1)}, u32[]{:S(2)}, u32[]{:S(2)}) %collective-permute-start.27) | collective-permute-done | bytes 131104 | tf_op jit(solution)/shard_map/ppermute | solution.py:35
  85.8 2.4 %collective-permute-done.28.refs_8_ = bf16[256,256]{1,0:T(8,128)(2,1)S(1)} collective-permute-done((bf16[256,256]{1,0:T(8,128)(2,1)S(1)}, bf16[256,256]{1,0:T(8,128)(2,1)S(1)}, u32[]{:S(2)}, u32[]{:S(2)}) %collective-permute-start.28) | collective-permute-done | bytes 131104 | tf_op jit(solution)/shard_map/ppermute | solution.py:35
  90.5 3.3 %all-to-all-start.2 = ((f32[4,32,256]{2,1,0:T(8,128)}), f32[4,32,256]{2,1,0:T(8,128)S(1)}, u32[]{:S(2)}, u32[]{:S(2)}) async-start(f32[4,32,256]{2,1,0:T(8,128)} %broadcast_in_dim.12), calls=%async_computation.2 | async-start | bytes 262144 | tf_op jit(solution)/shard_map/all_to_all | solution.py:320
  100.0 4.4 %all-to-all-start.3 = ((f32[8,32,256]{2,1,0:T(8,128)}), f32[8,32,256]{2,1,0:T(8,128)S(1)}, u32[]{:S(2)}, u32[]{:S(2)}) async-start(f32[8,32,256]{2,1,0:T(8,128)} %broadcast_in_dim.13), calls=%async_computation.3 | async-start | bytes 524288 | tf_op jit(solution)/shard_map/all_to_all | solution.py:320
  108.3 3.2 %early.3.refs_2_ = f32[256,256]{1,0:T(8,128)} custom-call(s32[64]{0:T(128)} %bitcast.30, bf16[64,128,128]{2,1,0:T(8,128)(2,1)} %bitcast.16, bf16[768,256]{1,0:T(8,128)(2,1)} %copy-done.3, bf16[768,256]{1,0:T(8,128)(2,1)} %copy-done.10, bf16[768,256]{1,0:T(8,128)(2,1)} %copy-done.8, bf16[512,256]{1,0:T(8,128)(2,1)} %copy-done.5, bf16[512,256]{1,0:T(8,128)(2,1)} %copy-done.14, ...), custom_call_target="tpu_custom_call" | custom-call | flops 268435456 | bytes 2359552 | tf_op jit(solution)/shard_map/early/pallas_call | solution.py:225
  111.5 2.3 %all-to-all-done.3 = f32[8,32,256]{2,1,0:T(8,128)S(1)} async-done(((f32[8,32,256]{2,1,0:T(8,128)}), f32[8,32,256]{2,1,0:T(8,128)S(1)}, u32[]{:S(2)}, u32[]{:S(2)}) %all-to-all-start.3) | async-done | bytes 262176 | tf_op jit(solution)/shard_map/all_to_all | solution.py:320
  113.9 2.4 %collective-permute-done.34.refs_11_ = bf16[512,256]{1,0:T(8,128)(2,1)} collective-permute-done((bf16[512,256]{1,0:T(8,128)(2,1)}, bf16[512,256]{1,0:T(8,128)(2,1)}, u32[]{:S(2)}, u32[]{:S(2)}) %collective-permute-start.34) | collective-permute-done | bytes 262176 | tf_op jit(solution)/shard_map/ppermute | solution.py:39
  117.0 9.6 %all-to-all-start.4 = ((f32[8,32,256]{2,1,0:T(8,128)}), f32[8,32,256]{2,1,0:T(8,128)S(1)}, u32[]{:S(2)}, u32[]{:S(2)}) async-start(f32[8,32,256]{2,1,0:T(8,128)} %broadcast_in_dim.28), calls=%async_computation.4 | async-start | bytes 524288 | tf_op jit(solution)/shard_map/all_to_all | solution.py:342
  126.6 4.1 %backward.1 = bf16[256,256]{1,0:T(8,128)(2,1)} custom-call(s32[64]{0:T(128)} %bitcast.31, bf16[64,128,128]{2,1,0:T(8,128)(2,1)} %bitcast.17, f32[256,256]{1,0:T(8,128)} %early.3.refs_2_, bf16[256,1024]{1,0:T(8,128)(2,1)} %get-tuple-element.38.refs_3_, bf16[8,192,256]{2,1,0:T(8,128)(2,1)} %copy-done, bf16[256,256]{1,0:T(8,128)(2,1)} %refs_5_.3, ...), custom_call_target="tpu_custom_call" | custom-call | flops 268435456 | bytes 3932416 | tf_op jit(solution)/shard_map/backward/pallas_call | solution.py:225
  130.7 2.4 %all-to-all-done.4 = f32[8,32,256]{2,1,0:T(8,128)S(1)} async-done(((f32[8,32,256]{2,1,0:T(8,128)}), f32[8,32,256]{2,1,0:T(8,128)S(1)}, u32[]{:S(2)}, u32[]{:S(2)}) %all-to-all-start.4) | async-done | bytes 262176 | tf_op jit(solution)/shard_map/all_to_all | solution.py:342
  (138 shorter events, 40.8 us)
Async XLA Ops:
  12.6 10.1 %collective-permute-start.2 = (bf16[768,256]{1,0:T(8,128)(2,1)S(1)}, bf16[768,256]{1,0:T(8,128)(2,1)S(1)}, u32[]{:S(2)}, u32[]{:S(2)}) collective-permute-start(bf16[768,256]{1,0:T(8,128)(2,1)S(1)} %pad_maximum_fusion.refs_2_), channel_id=1, source_target_pairs={{0,64},{8,72},{16,80},{24,88},{32,96},{40,104},{48,112},{56,120},{... | collective-permute-start | bytes 1179656 | tf_op jit(solution)/shard_map/ppermute | solution.py:39
  13.9 22.5 %collective-permute-start.3 = (bf16[768,256]{1,0:T(8,128)(2,1)S(1)}, bf16[768,256]{1,0:T(8,128)(2,1)S(1)}, u32[]{:S(2)}, u32[]{:S(2)}) collective-permute-start(bf16[768,256]{1,0:T(8,128)(2,1)S(1)} %pad_maximum_fusion.refs_2_), channel_id=1, source_target_pairs={{0,192},{8,200},{16,208},{24,216},{32,224},{40,232},{48,240},{56,2... | collective-permute-start | bytes 1179656 | tf_op jit(solution)/shard_map/ppermute | solution.py:39
  18.7 19.1 %collective-permute-start.6 = (bf16[512,256]{1,0:T(8,128)(2,1)S(1)}, bf16[512,256]{1,0:T(8,128)(2,1)S(1)}, u32[]{:S(2)}, u32[]{:S(2)}) collective-permute-start(bf16[512,256]{1,0:T(8,128)(2,1)S(1)} %constant_dynamic-update-slice_fusion.refs_5_), channel_id=1, source_target_pairs={{0,64},{8,72},{16,80},{24,88},{32,96},{40,104},{48,112},{56,120},{... | collective-permute-start | bytes 786440 | tf_op jit(solution)/shard_map/ppermute | solution.py:39
  19.9 22.0 %collective-permute-start.7 = (bf16[512,256]{1,0:T(8,128)(2,1)S(1)}, bf16[512,256]{1,0:T(8,128)(2,1)}, u32[]{:S(2)}, u32[]{:S(2)}) collective-permute-start(bf16[512,256]{1,0:T(8,128)(2,1)S(1)} %constant_dynamic-update-slice_fusion.refs_5_), channel_id=1, source_target_pairs={{0,192},{8,200},{16,208},{24,216},{32,224},{40,232},{48,240},{56,2... | collective-permute-start | bytes 786440 | tf_op jit(solution)/shard_map/ppermute | solution.py:39
  22.7 19.8 %collective-permute-start.13 = (bf16[512,256]{1,0:T(8,128)(2,1)S(1)}, bf16[512,256]{1,0:T(8,128)(2,1)S(1)}, u32[]{:S(2)}, u32[]{:S(2)}) collective-permute-start(bf16[512,256]{1,0:T(8,128)(2,1)S(1)} %constant_dynamic-update-slice_fusion.2.refs_9_), channel_id=1, source_target_pairs={{0,64},{8,72},{16,80},{24,88},{32,96},{40,104},{48,112},{56,120},{... | collective-permute-start | bytes 786440 | tf_op jit(solution)/shard_map/ppermute | solution.py:39
  22.8 21.7 %collective-permute-start.14 = (bf16[512,256]{1,0:T(8,128)(2,1)S(1)}, bf16[512,256]{1,0:T(8,128)(2,1)S(1)}, u32[]{:S(2)}, u32[]{:S(2)}) collective-permute-start(bf16[512,256]{1,0:T(8,128)(2,1)S(1)} %constant_dynamic-update-slice_fusion.2.refs_9_), channel_id=1, source_target_pairs={{0,192},{8,200},{16,208},{24,216},{32,224},{40,232},{48,240},{56,2... | collective-permute-start | bytes 786440 | tf_op jit(solution)/shard_map/ppermute | solution.py:39
  26.2 25.8 %all-to-all-start = ((bf16[8,128,256]{2,1,0:T(8,128)(2,1)}), bf16[8,128,256]{2,1,0:T(8,128)(2,1)S(1)}, u32[]{:S(2)}, u32[]{:S(2)}) async-start(bf16[8,128,256]{2,1,0:T(8,128)(2,1)} %get-tuple-element.26), calls=%async_computation | async-start | bytes 1048576 | tf_op jit(solution)/shard_map/all_to_all | solution.py:261
  37.8 19.1 %collective-permute-start.10 = (bf16[768,256]{1,0:T(8,128)(2,1)S(1)}, bf16[768,256]{1,0:T(8,128)(2,1)S(1)}, u32[]{:S(2)}, u32[]{:S(2)}) collective-permute-start(bf16[768,256]{1,0:T(8,128)(2,1)S(1)} %collective-permute-done.3.refs_4_), channel_id=1, source_target_pairs={{0,64},{8,72},{16,80},{24,88},{32,96},{40,104},{48,112},{56,120},{... | collective-permute-start | bytes 1179656 | tf_op jit(solution)/shard_map/ppermute | solution.py:39
  41.6 9.5 %collective-permute-start.16 = (bf16[256,256]{1,0:T(8,128)(2,1)S(1)}, bf16[256,256]{1,0:T(8,128)(2,1)S(1)}, u32[]{:S(2)}, u32[]{:S(2)}) collective-permute-start(bf16[256,256]{1,0:T(8,128)(2,1)S(1)} %collective-permute-done.9.refs_8_), channel_id=1, source_target_pairs={{0,64},{8,72},{16,80},{24,88},{32,96},{40,104},{48,112},{56,120},{... | collective-permute-start | bytes 393224 | tf_op jit(solution)/shard_map/ppermute | solution.py:39
  42.5 13.3 %collective-permute-start.11 = (bf16[512,256]{1,0:T(8,128)(2,1)S(1)}, bf16[512,256]{1,0:T(8,128)(2,1)}, u32[]{:S(2)}, u32[]{:S(2)}) collective-permute-start(bf16[512,256]{1,0:T(8,128)(2,1)S(1)} %collective-permute-done.6.refs_6_), channel_id=1, source_target_pairs={{0,192},{8,200},{16,208},{24,216},{32,224},{40,232},{48,240},{56,2... | collective-permute-start | bytes 786440 | tf_op jit(solution)/shard_map/ppermute | solution.py:39
  44.5 12.4 %collective-permute-start.15 = (bf16[512,256]{1,0:T(8,128)(2,1)S(1)}, bf16[512,256]{1,0:T(8,128)(2,1)}, u32[]{:S(2)}, u32[]{:S(2)}) collective-permute-start(bf16[512,256]{1,0:T(8,128)(2,1)S(1)} %collective-permute-done.14.refs_11_), channel_id=1, source_target_pairs={{0,64},{8,72},{16,80},{24,88},{32,96},{40,104},{48,112},{56,120},{... | collective-permute-start | bytes 786440 | tf_op jit(solution)/shard_map/ppermute | solution.py:39
  62.5 9.7 %collective-permute-start.20 = (bf16[256,256]{1,0:T(8,128)(2,1)}, bf16[256,256]{1,0:T(8,128)(2,1)S(1)}, u32[]{:S(2)}, u32[]{:S(2)}) collective-permute-start(bf16[256,256]{1,0:T(8,128)(2,1)} %get-tuple-element.37), channel_id=1, source_target_pairs={{0,56},{8,16},{16,8},{24,32},{32,24},{40,48},{48,40},{56,0},{64,12... | collective-permute-start | bytes 393224 | tf_op jit(solution)/shard_map/ppermute | solution.py:35
  64.3 10.7 %collective-permute-start.19 = (bf16[256,256]{1,0:T(8,128)(2,1)}, bf16[256,256]{1,0:T(8,128)(2,1)S(1)}, u32[]{:S(2)}, u32[]{:S(2)}) collective-permute-start(bf16[256,256]{1,0:T(8,128)(2,1)} %get-tuple-element.37), channel_id=1, source_target_pairs={{0,8},{8,0},{16,24},{24,16},{32,40},{40,32},{48,56},{56,48},{64,72... | collective-permute-start | bytes 393224 | tf_op jit(solution)/shard_map/ppermute | solution.py:35
  64.3 23.9 %all-to-all-start.1 = ((bf16[8,192,256]{2,1,0:T(8,128)(2,1)}), bf16[8,192,256]{2,1,0:T(8,128)(2,1)S(1)}, u32[]{:S(2)}, u32[]{:S(2)}) async-start(bf16[8,192,256]{2,1,0:T(8,128)(2,1)} %get-tuple-element.39), calls=%async_computation.1 | async-start | bytes 1572864 | tf_op jit(solution)/shard_map/all_to_all | solution.py:314
  78.8 9.7 %collective-permute-start.21 = (bf16[768,256]{1,0:T(8,128)(2,1)S(1)}, bf16[768,256]{1,0:T(8,128)(2,1)S(1)}, u32[]{:S(2)}, u32[]{:S(2)}) collective-permute-start(bf16[768,256]{1,0:T(8,128)(2,1)S(1)} %constant_dynamic-update-slice_fusion.4.refs_2_), channel_id=1, source_target_pairs={{0,64},{8,72},{16,80},{24,88},{32,96},{40,104},{48,112},{56,120},{... | collective-permute-start | bytes 1179656 | tf_op jit(solution)/shard_map/ppermute | solution.py:39
  78.9 10.9 %collective-permute-start.22 = (bf16[768,256]{1,0:T(8,128)(2,1)S(1)}, bf16[768,256]{1,0:T(8,128)(2,1)S(1)}, u32[]{:S(2)}, u32[]{:S(2)}) collective-permute-start(bf16[768,256]{1,0:T(8,128)(2,1)S(1)} %constant_dynamic-update-slice_fusion.4.refs_2_), channel_id=1, source_target_pairs={{0,192},{8,200},{16,208},{24,216},{32,224},{40,232},{48,240},{56,2... | collective-permute-start | bytes 1179656 | tf_op jit(solution)/shard_map/ppermute | solution.py:39
  83.5 20.9 %collective-permute-start.25 = (bf16[512,256]{1,0:T(8,128)(2,1)S(1)}, bf16[512,256]{1,0:T(8,128)(2,1)S(1)}, u32[]{:S(2)}, u32[]{:S(2)}) collective-permute-start(bf16[512,256]{1,0:T(8,128)(2,1)S(1)} %constant_dynamic-update-slice_fusion.7.refs_5_), channel_id=1, source_target_pairs={{0,64},{8,72},{16,80},{24,88},{32,96},{40,104},{48,112},{56,120},{... | collective-permute-start | bytes 786440 | tf_op jit(solution)/shard_map/ppermute | solution.py:39
  85.1 19.3 %collective-permute-start.26 = (bf16[512,256]{1,0:T(8,128)(2,1)S(1)}, bf16[512,256]{1,0:T(8,128)(2,1)}, u32[]{:S(2)}, u32[]{:S(2)}) collective-permute-start(bf16[512,256]{1,0:T(8,128)(2,1)S(1)} %constant_dynamic-update-slice_fusion.7.refs_5_), channel_id=1, source_target_pairs={{0,192},{8,200},{16,208},{24,216},{32,224},{40,232},{48,240},{56,2... | collective-permute-start | bytes 786440 | tf_op jit(solution)/shard_map/ppermute | solution.py:39
  88.5 10.8 %collective-permute-start.36 = (bf16[256,256]{1,0:T(8,128)(2,1)S(1)}, bf16[256,256]{1,0:T(8,128)(2,1)S(1)}, u32[]{:S(2)}, u32[]{:S(2)}) collective-permute-start(bf16[256,256]{1,0:T(8,128)(2,1)S(1)} %collective-permute-done.28.refs_8_), channel_id=1, source_target_pairs={{0,192},{8,200},{16,208},{24,216},{32,224},{40,232},{48,240},{56,2... | collective-permute-start | bytes 393224 | tf_op jit(solution)/shard_map/ppermute | solution.py:39
  93.8 12.1 %collective-permute-start.32 = (bf16[512,256]{1,0:T(8,128)(2,1)S(1)}, bf16[512,256]{1,0:T(8,128)(2,1)}, u32[]{:S(2)}, u32[]{:S(2)}) collective-permute-start(bf16[512,256]{1,0:T(8,128)(2,1)S(1)} %constant_dynamic-update-slice_fusion.9.refs_8_), channel_id=1, source_target_pairs={{0,64},{8,72},{16,80},{24,88},{32,96},{40,104},{48,112},{56,120},{... | collective-permute-start | bytes 786440 | tf_op jit(solution)/shard_map/ppermute | solution.py:39
  100.0 13.8 %all-to-all-start.3 = ((f32[8,32,256]{2,1,0:T(8,128)}), f32[8,32,256]{2,1,0:T(8,128)S(1)}, u32[]{:S(2)}, u32[]{:S(2)}) async-start(f32[8,32,256]{2,1,0:T(8,128)} %broadcast_in_dim.13), calls=%async_computation.3 | async-start | bytes 524288 | tf_op jit(solution)/shard_map/all_to_all | solution.py:320
  104.4 9.5 %collective-permute-start.29 = (bf16[768,256]{1,0:T(8,128)(2,1)S(1)}, bf16[768,256]{1,0:T(8,128)(2,1)S(1)}, u32[]{:S(2)}, u32[]{:S(2)}) collective-permute-start(bf16[768,256]{1,0:T(8,128)(2,1)S(1)} %collective-permute-done.22.refs_4_), channel_id=1, source_target_pairs={{0,64},{8,72},{16,80},{24,88},{32,96},{40,104},{48,112},{56,120},{... | collective-permute-start | bytes 1179656 | tf_op jit(solution)/shard_map/ppermute | solution.py:39
  106.0 10.3 %collective-permute-start.34 = (bf16[512,256]{1,0:T(8,128)(2,1)}, bf16[512,256]{1,0:T(8,128)(2,1)}, u32[]{:S(2)}, u32[]{:S(2)}) collective-permute-start(bf16[512,256]{1,0:T(8,128)(2,1)} %collective-permute-done.33.refs_10_), channel_id=1, source_target_pairs={{0,64},{8,72},{16,80},{24,88},{32,96},{40,104},{48,112},{56,120},{... | collective-permute-start | bytes 786440 | tf_op jit(solution)/shard_map/ppermute | solution.py:39
  117.0 16.2 %all-to-all-start.4 = ((f32[8,32,256]{2,1,0:T(8,128)}), f32[8,32,256]{2,1,0:T(8,128)S(1)}, u32[]{:S(2)}, u32[]{:S(2)}) async-start(f32[8,32,256]{2,1,0:T(8,128)} %broadcast_in_dim.28), calls=%async_computation.4 | async-start | bytes 524288 | tf_op jit(solution)/shard_map/all_to_all | solution.py:342
  (44 other events, 444.6 us)
